TPU v7x, 32 devices: a whole 2x2x4 slice. The times are simulated.
32 devices in a mesh: mem: 2 (over core), lat: 16 (over z, y, x).
Axes of the slice: x: 2, y: 2, z: 4, core: 2. Of those that a mesh axis runs over, the one named last changes fastest.
Arguments:
- perturbations: bfloat16 [32, 2, 4, 64, 1440], P('mem', None, None, 'lat'), may hold values from -1 to 1
- gradient_held: float32 [2, 4, 64, 1440], P(None, 'mem', 'lat'), may hold values from -6 to 6
- block_owner: int32 [4], replicated, may hold values from 0 to 3, each once
Outputs:
- increment_held: float32 [2, 4, 64, 1440], P(None, 'mem', 'lat')
Inputs may be any that keep to these rules, and one draw needn't show every extreme that they name: `block_owner`: each value appears exactly once.
All inputs are finite; a program needn't handle non-finite values.
Results may differ from a plain program's by a relative error of at most 0.0022.
Values may be sent and summed in bfloat16 or wider, within the bound.
A program may use at most 128 MiB of HBM per device.

v0:
```python
import math

import jax
import jax.numpy as jnp
from jax import lax
from jax.sharding import PartitionSpec as P


def extended_2(block, sides, width):
    for axis, dim in sides:
        count = lax.axis_size(axis)
        forward = [(i, i + 1) for i in range(count - 1)]
        backward = [(target, source) for source, target in forward]
        low = lax.ppermute(
            lax.slice_in_dim(block, block.shape[dim] - width, None, axis=dim), axis, forward
        )
        high = lax.ppermute(lax.slice_in_dim(block, 0, width, axis=dim), axis, backward)
        block = jnp.concatenate([low, block, high], axis=dim)
    return block


def weights_for(spread_cells):
    return [
        math.exp(-(offset * offset) / (2.0 * spread_cells * spread_cells))
        for offset in range(-4, 5)
    ]


def smooth_periodic(source, along_dim, weights):
    summed = jnp.zeros_like(source)
    for offset in range(-4, 5):
        summed = summed + weights[offset + 4] * jnp.roll(source, -offset, axis=along_dim)
    return summed


def smooth_bounded(source, along_dim, weights):
    length = source.shape[along_dim]
    widths = [(0, 0)] * source.ndim
    widths[along_dim] = (4, 4)
    padded = jnp.pad(source, widths)
    summed = jnp.zeros_like(source)
    for offset in range(-4, 5):
        summed = summed + weights[offset + 4] * lax.slice_in_dim(
            padded, 4 + offset, 4 + offset + length, axis=along_dim
        )
    return summed


def lat_rows(extended, weights, rows_here):
    summed = jnp.zeros(extended.shape[:1] + (rows_here,) + extended.shape[2:], jnp.float32)
    for offset in range(-4, 5):
        summed = summed + weights[offset + 4] * lax.slice_in_dim(
            extended, 4 + offset, 4 + offset + rows_here, axis=1
        )
    return summed


def local(perturbations, gradient_held, block_owner):
    gathered = lax.all_gather(gradient_held, "mem", axis=1, tiled=True)
    slot_count, levels, rows_here, lon_count = gathered.shape
    places = jnp.arange(levels, dtype=jnp.int32)
    inverse = jnp.sum(
        jnp.where(block_owner[None, :] == places[:, None], places[None, :], 0), axis=1
    )
    gradient = jnp.take(gathered, inverse, axis=1)
    lon_weights = weights_for(3.0)
    lev_weights = weights_for(2.0)
    lat_weights = weights_for(2.5)

    def lon_lev(field):
        smoothed_part = smooth_periodic(field.astype(jnp.float32), 2, lon_weights)
        return smooth_bounded(smoothed_part, 0, lev_weights)

    control = perturbations[:, 0].astype(jnp.float32) * gradient[0]
    control = control + perturbations[:, 1].astype(jnp.float32) * gradient[1]
    control = control.astype(jnp.bfloat16)
    start = jnp.zeros((slot_count, levels, rows_here, lon_count), jnp.float32)
    extended = extended_2(control, (("lat", 2),), 4)

    def member_step(summed, pair):
        rows_ext, member = pair
        smoothed = lat_rows(lon_lev(rows_ext), lat_weights, rows_here)
        return (summed + member.astype(jnp.float32) * smoothed[None], None)

    increment_terms, unused = lax.scan(member_step, start, (extended, perturbations))
    ordered = jnp.take(increment_terms, block_owner, axis=1)
    return lax.psum_scatter(ordered, "mem", scatter_dimension=1, tiled=True)


def solution(mesh):
    placed = (P("mem", None, None, "lat", None), P(None, "mem", "lat", None), P())
    return jax.shard_map(
        local, mesh=mesh, in_specs=placed, out_specs=P(None, "mem", "lat", None), check_vma=False
    )
```

profile of v0, /device:TPU:25, one launch (start us, length us, event | category | flops | bytes accessed | tf_op | source)
XLA Modules:
  0.0 132.5 jit_solution(15663955990900319161)
XLA Ops:
  6.5 0.8 select_reduce_fusion
  7.4 2.6 %all_gather.3 = f32[2,4,4,1440]{3,2,1,0:T(4,128)S(1)} all-gather(f32[2,2,4,1440]{3,2,1,0:T(4,128)} %param.8), channel_id=1, replica_groups=mesh['mem'=2,'lat'=16] {'mem'}, dimensions={1}, use_global_device_ids=true | all-gather | bytes 276480 | tf_op jit(solution)/shard_map/all_gather | solution.py:59
  10.0 0.7 gather_fusion
  10.8 2.0 %fusion.29 = bf16[16,4,4,1440]{3,2,1,0:T(4,128)(2,1)S(1)} fusion(f32[4,4,1440]{2,1,0:T(4,128)S(1)} %get-tuple-element.115, bf16[16,2,4,4,1440]{4,3,2,1,0:T(4,128)(2,1)} %param.7, f32[4,4,1440]{2,1,0:T(4,128)S(1)} %get-tuple-element.114), kind=kLoop, calls=%fused_computation.58 | loop fusion | flops 2211840 | bytes 2396160 | tf_op jit(solution)/shard_map/convert_element_type | solution.py:76
  12.8 3.1 %collective-permute-start = (bf16[16,4,4,1440]{3,2,1,0:T(4,128)(2,1)S(1)}, bf16[16,4,4,1440]{3,2,1,0:T(4,128)(2,1)S(1)}, u32[]{:S(2)}, u32[]{:S(2)}) collective-permute-start(bf16[16,4,4,1440]{3,2,1,0:T(4,128)(2,1)S(1)} %fusion.29), channel_id=1, source_target_pairs={{0,1},{1,2},{2,3},{3,4},{4,5},{5,6},{6,7},{7,8},{8,9},{9,10},{10,1... | collective-permute-start | bytes 2211848 | tf_op jit(solution)/shard_map/ppermute | solution.py:14
  16.0 4.0 %collective-permute-start.1 = (bf16[16,4,4,1440]{3,2,1,0:T(4,128)(2,1)S(1)}, bf16[16,4,4,1440]{3,2,1,0:T(4,128)(2,1)}, u32[]{:S(2)}, u32[]{:S(2)}) collective-permute-start(bf16[16,4,4,1440]{3,2,1,0:T(4,128)(2,1)S(1)} %fusion.29), channel_id=1, source_target_pairs={{1,0},{2,1},{3,2},{4,3},{5,4},{6,5},{7,6},{8,7},{9,8},{10,9},{11,1... | collective-permute-start | bytes 2211848 | tf_op jit(solution)/shard_map/ppermute | solution.py:17
  20.0 15.4 %collective-permute-done = bf16[16,4,4,1440]{3,2,1,0:T(4,128)(2,1)S(1)} collective-permute-done((bf16[16,4,4,1440]{3,2,1,0:T(4,128)(2,1)S(1)}, bf16[16,4,4,1440]{3,2,1,0:T(4,128)(2,1)S(1)}, u32[]{:S(2)}, u32[]{:S(2)}) %collective-permute-start) | collective-permute-done | bytes 737312 | tf_op jit(solution)/shard_map/ppermute | solution.py:14
  35.3 0.9 copy-done.1
  36.2 15.2 %collective-permute-done.1 = bf16[16,4,4,1440]{3,2,1,0:T(4,128)(2,1)} collective-permute-done((bf16[16,4,4,1440]{3,2,1,0:T(4,128)(2,1)S(1)}, bf16[16,4,4,1440]{3,2,1,0:T(4,128)(2,1)}, u32[]{:S(2)}, u32[]{:S(2)}) %collective-permute-start.1) | collective-permute-done | bytes 737312 | tf_op jit(solution)/shard_map/ppermute | solution.py:17
  51.4 3.3 %pad_maximum_fusion = bf16[16,4,12,1440]{3,2,1,0:T(8,128)(2,1)S(1)} fusion(bf16[16,4,4,1440]{3,2,1,0:T(4,128)(2,1)} %collective-permute-done.1, bf16[16,4,4,1440]{3,2,1,0:T(4,128)(2,1)} %copy-done, bf16[16,4,4,1440]{3,2,1,0:T(4,128)(2,1)} %copy-done.1), kind=kLoop, calls=%fused_computation.55 | loop fusion | flops 6635520 | bytes 4423680 | tf_op jit(solution)/shard_map/concatenate | solution.py:18
  54.7 48.5 %while.14 = (s32[]{:T(128)}, f32[2,4,4,1440]{3,2,1,0:T(4,128)S(1)}, bf16[16,2,4,4,1440]{4,3,2,1,0:T(4,128)(2,1)}, bf16[16,4,12,1440]{3,2,1,0:T(8,128)(2,1)S(1)}, s32[]{:T(128)}, /*index=5*/s32[]{:T(128)}) while((s32[]{:T(128)}, f32[2,4,4,1440]{3,2,1,0:T(4,128)S(1)}, bf16[16,2,4,4,1440]{4,3,2,1,0:T(4,128)(2,1)}, ...), condition=%wide.region_2.4_spmd.clone, body=%wide.region_1.3_spmd.clone.sunk | while | flops 3179523 | bytes 9492571 | solution.py:85
  55.8 0.6 fusion.58
  56.4 0.2 fusion.60
  56.6 1.1 fusion.61
  58.8 0.6 fusion.58
  59.5 0.2 fusion.60
  59.7 1.1 fusion.61
  61.8 0.6 fusion.58
  62.5 0.2 fusion.60
  62.7 1.1 fusion.61
  64.8 0.6 fusion.58
  65.5 0.2 fusion.60
  65.7 1.1 fusion.61
  67.9 0.6 fusion.58
  68.5 0.2 fusion.60
  68.8 1.1 fusion.61
  70.9 0.6 fusion.58
  71.6 0.2 fusion.60
  71.8 1.1 fusion.61
  73.9 0.6 fusion.58
  74.6 0.2 fusion.60
  74.8 1.1 fusion.61
  76.9 0.6 fusion.58
  77.6 0.2 fusion.60
  77.8 1.1 fusion.61
  80.0 0.6 fusion.58
  80.7 0.2 fusion.60
  80.9 1.1 fusion.61
  83.0 0.6 fusion.58
  83.7 0.2 fusion.60
  83.9 1.1 fusion.61
  86.0 0.6 fusion.58
  86.7 0.2 fusion.60
  86.9 1.1 fusion.61
  89.1 0.6 fusion.58
  89.7 0.2 fusion.60
  90.0 1.1 fusion.61
  92.1 0.6 fusion.58
  92.8 0.2 fusion.60
  93.0 1.1 fusion.61
  95.1 0.6 fusion.58
  95.8 0.2 fusion.60
  96.0 1.1 fusion.61
  98.1 0.6 fusion.58
  98.8 0.2 fusion.60
  99.0 1.1 fusion.61
  101.2 0.6 fusion.58
  102.1 1.1 fusion.61
  103.2 0.7 gather_fusion.1
  103.8 0.8 select_bitcast_fusion
  104.7 0.6 dynamic-slice
  105.9 18.2 %all-reduce.4.cloned.1.call-done = f32[2,4,4,1440]{3,2,0,1:T(4,128)} async-done(((f32[2,4,4,1440]{3,2,0,1:T(4,128)}), f32[2,4,4,1440]{3,2,0,1:T(4,128)}) %all-reduce.4.cloned.1.call-update) | async-done | bytes 184336
  124.1 0.9 constant_dynamic-slice_fusion
  125.0 0.6 copy.14
  (179 shorter events, 18.1 us)
Async XLA Ops:
  6.5 13.4 %copy-start.2 = (s32[4]{0:T(128)S(1)}, s32[4]{0:T(128)}, u32[]{:S(2)}) copy-start(s32[4]{0:T(128)} %param.9) | copy-start | bytes 52
  6.5 117.6 %all-reduce.4.cloned.1.call-start = ((), (), s32[]{:S(2)}) async-start(), calls=%async_computation | async-start | bytes 393216
  12.8 22.5 %copy-start = (bf16[16,4,4,1440]{3,2,1,0:T(4,128)(2,1)}, bf16[16,4,4,1440]{3,2,1,0:T(4,128)(2,1)S(1)}, u32[]{:S(2)}) copy-start(bf16[16,4,4,1440]{3,2,1,0:T(4,128)(2,1)S(1)} %fusion.29) | copy-start | bytes 2211844
  12.8 22.5 %collective-permute-start = (bf16[16,4,4,1440]{3,2,1,0:T(4,128)(2,1)S(1)}, bf16[16,4,4,1440]{3,2,1,0:T(4,128)(2,1)S(1)}, u32[]{:S(2)}, u32[]{:S(2)}) collective-permute-start(bf16[16,4,4,1440]{3,2,1,0:T(4,128)(2,1)S(1)} %fusion.29), channel_id=1, source_target_pairs={{0,1},{1,2},{2,3},{3,4},{4,5},{5,6},{6,7},{7,8},{8,9},{9,10},{10,1... | collective-permute-start | bytes 2211848 | tf_op jit(solution)/shard_map/ppermute | solution.py:14
  16.0 35.5 %collective-permute-start.1 = (bf16[16,4,4,1440]{3,2,1,0:T(4,128)(2,1)S(1)}, bf16[16,4,4,1440]{3,2,1,0:T(4,128)(2,1)}, u32[]{:S(2)}, u32[]{:S(2)}) collective-permute-start(bf16[16,4,4,1440]{3,2,1,0:T(4,128)(2,1)S(1)} %fusion.29), channel_id=1, source_target_pairs={{1,0},{2,1},{3,2},{4,3},{5,4},{6,5},{7,6},{8,7},{9,8},{10,9},{11,1... | collective-permute-start | bytes 2211848 | tf_op jit(solution)/shard_map/ppermute | solution.py:17
  35.3 0.9 copy-start.1
  54.7 50.0 %copy-start.3 = (u32[32]{0:T(128)S(1)}, u32[32]{0:T(128)}, u32[]{:S(2)}) copy-start(u32[32]{0:T(128)} %constant.110) | copy-start | bytes 388
Sparse Core Ops, SparseCore 0:
  104.8 19.3 all-reduce.3
where the time goes:
time: 134 us; the launch traced here: 133 us
  waiting for transfers between devices  48.8 us (36%)
  other arithmetic  39 us (29%)
  local copies, waits for them, and re-layouts  20.2 us (15%)
  between operations  14.2 us (11%)
  starting transfers between devices  7.08 us (5%)
  blocking collectives  2.59 us (2%)
    unnamed x2, waiting for transfers between devices  18.2 us
    add x16, other arithmetic, member_step(): return (summed + member.astype(jnp.float32) * smoothed[None], None)  17.5 us
    slice x128, local copies, waits for them, and re-layouts, smooth_periodic(): jnp.roll(source, -offset, axis=along_dim)  15.8 us
    ppermute x1, waiting for transfers between devices, extended_2(): lax.ppermute(lax.slice_in_dim(block, block.shape[dim] - width, None, axis...  15.4 us
    ppermute x1, waiting for transfers between devices, extended_2(): lax.ppermute(lax.slice_in_dim(block, 0, width, axis=dim), axis, backward)  15.2 us
    add x16, other arithmetic, smooth_periodic(): summed + weights[offset + 4] * jnp.roll(source, -offset, axis=along_dim)  9.33 us
    ppermute x1, starting transfers between devices, extended_2(): lax.ppermute(lax.slice_in_dim(block, 0, width, axis=dim), axis, backward)  3.96 us
    concatenate x1, other arithmetic, extended_2(): block = jnp.concatenate([low, block, high], axis=dim)  3.27 us
  transfers between devices with their start and end apart: 3, of which 3 were waited for; matrix products, arithmetic and copies ran while one was open for 0% of the time, Pallas kernels for 0%

commit v1 on v0

v1 whole, which is shorter than its diff:
```python
import functools
import math

import jax
import jax.numpy as jnp
import ml_dtypes
import numpy as np
from jax import lax
from jax.experimental import pallas as pl
from jax.experimental.pallas import tpu as pltpu
from jax.sharding import PartitionSpec as P

MESH = pl.DeviceIdType.MESH
REACH = 4
EDGE = 128
TILE = 256
F32 = jnp.float32
BF16 = jnp.bfloat16


def rho(offset, spread):
    if abs(offset) > REACH:
        return 0.0
    return math.exp(-(offset * offset) / (2.0 * spread * spread))


def split_weights(exact):
    high = exact.astype(ml_dtypes.bfloat16)
    low = (exact - high.astype(np.float64)).astype(ml_dtypes.bfloat16)
    return high, low


def level_row_weights(levels, rows, group):
    lev = np.array([[rho(a - b, 2.0) for b in range(levels)] for a in range(levels)])

    def block(shift):
        lat = np.array([[rho(b + shift * rows - a, 2.5) for b in range(rows)] for a in range(rows)])
        return np.kron(np.eye(group), np.kron(lev, lat))

    both = []
    for direct in (1, -1):
        high, low = split_weights(np.concatenate([block(0), block(direct), block(-direct)], axis=1))
        both.append(np.concatenate([high, low], axis=0))
    return np.stack(both)


def fill_lon_weights(wlon):
    shape = wlon.shape[1:]
    inward = lax.broadcasted_iota(jnp.int32, shape, 0)
    outward = lax.broadcasted_iota(jnp.int32, shape, 1)
    apart = jnp.abs(inward - EDGE - outward)
    halves = split_weights(np.array([rho(a, 3.0) for a in range(REACH + 1)]))
    for half in range(2):
        band = jnp.zeros(shape, F32)
        for a in range(REACH + 1):
            band = jnp.where(apart == a, float(halves[half][a]), band)
        wlon[half] = band.astype(BF16)


def kernel(
    group, owner, pert, held, wlat, out,
    wlon, gbuf, gord, cbuf, dbuf, rbuf, total, levelled, give, take,
    g_send, g_recv, c_send, c_recv, f_send, f_recv, t_send, t_recv,
):
    members, slots, depth, lon = pert.shape
    holders, _, held_levels, rows, _ = gbuf.shape
    levels = depth // rows
    chunks = members // group
    tiles = -(-lon // TILE)
    right_pad = tiles * TILE + EDGE - lon

    me = lax.axis_index("mem")
    here = lax.axis_index("lat")
    count = lax.axis_size("lat")
    parity = lax.rem(here, 2)
    partner = here + 1 - 2 * parity
    hop = 2 - 4 * parity
    target = here + hop
    source = here - hop
    has_target = jnp.logical_and(target >= 0, target < count)
    has_source = jnp.logical_and(source >= 0, source < count)

    barrier = pltpu.get_barrier_semaphore()
    for k in range(1, holders):
        pl.semaphore_signal(
            barrier, inc=1, device_id=(lax.rem(me + k, holders), here), device_id_type=MESH
        )
    pl.semaphore_signal(barrier, inc=1, device_id=(me, partner), device_id_type=MESH)

    @pl.when(has_target)
    def _():
        pl.semaphore_signal(barrier, inc=1, device_id=(me, target), device_id_type=MESH)

    @pl.when(has_source)
    def _():
        pl.semaphore_signal(barrier, inc=1, device_id=(me, source), device_id_type=MESH)

    pl.semaphore_wait(barrier, holders + has_target.astype(jnp.int32) + has_source.astype(jnp.int32))

    def gradient_copy(k):
        return pltpu.make_async_remote_copy(
            src_ref=held, dst_ref=gbuf.at[me],
            send_sem=g_send.at[k - 1], recv_sem=g_recv.at[k - 1],
            device_id=(lax.rem(me + k, holders), here), device_id_type=MESH,
        )

    for k in range(1, holders):
        gradient_copy(k).start()
    gbuf[me] = held[...]
    fill_lon_weights(wlon)

    @pl.when(jnp.logical_not(has_source))
    def _():
        rbuf[...] = jnp.zeros_like(rbuf)

    total[...] = jnp.zeros_like(total)
    for k in range(1, holders):
        gradient_copy(k).wait()

    for level in range(levels):
        place = jnp.int32(0)
        for p in range(levels):
            place = jnp.where(owner[p] == level, p, place)
        holder = lax.div(place, held_levels)
        within = lax.rem(place, held_levels)
        for slot in range(slots):
            gord[slot, level * rows:(level + 1) * rows, :] = gbuf[holder, slot, within]

    def own_copy(c):
        span = pl.ds(c * group, group)
        return pltpu.make_async_remote_copy(
            src_ref=cbuf.at[span], dst_ref=dbuf.at[span],
            send_sem=c_send.at[c], recv_sem=c_recv.at[c],
            device_id=(me, partner), device_id_type=MESH,
        )

    def relay_copy(c):
        span = pl.ds(c * group, group)
        return pltpu.make_async_remote_copy(
            src_ref=dbuf.at[span], dst_ref=rbuf.at[span],
            send_sem=f_send.at[c], recv_sem=f_recv.at[c],
            device_id=(me, target), device_id_type=MESH,
        )

    def control_step(c, carry):
        for i in range(group):
            m = c * group + i
            value = pert[m, 0].astype(F32) * gord[0]
            for slot in range(1, slots):
                value = value + pert[m, slot].astype(F32) * gord[slot]
            cbuf[m] = value.astype(BF16)
        own_copy(c).start()
        return carry

    lax.fori_loop(0, chunks, control_step, 0)

    def relay(c):
        own_copy(c).wait_recv()

        @pl.when(has_target)
        def _():
            relay_copy(c).start()

    def process(c):
        @pl.when(has_source)
        def _():
            relay_copy(c).wait_recv()

        span = pl.ds(c * group, group)
        block = group * depth
        stack = jnp.concatenate(
            [buf[span].reshape(block, lon) for buf in (cbuf, dbuf, rbuf)], axis=0
        )
        mixed = jnp.dot(wlat[parity], stack, preferred_element_type=F32)
        mixed = mixed[:block] + mixed[block:]
        ringed = jnp.concatenate(
            [mixed[:, lon - EDGE:], mixed, mixed[:, :right_pad]], axis=1
        )
        high = ringed.astype(BF16)
        low = (ringed - high.astype(F32)).astype(BF16)
        width = TILE + 2 * EDGE
        highs = [high[:, t * TILE:t * TILE + width] for t in range(tiles)]
        lows = [low[:, t * TILE:t * TILE + width] for t in range(tiles)]
        first = jnp.dot(
            jnp.concatenate(highs + lows, axis=0), wlon[0], preferred_element_type=F32
        )
        second = jnp.dot(jnp.concatenate(highs, axis=0), wlon[1], preferred_element_type=F32)
        smoothed = first[:tiles * block] + first[tiles * block:] + second
        for t in range(tiles):
            low_lon, high_lon = t * TILE, min((t + 1) * TILE, lon)
            for slot in range(slots):
                summed = total[slot, :, low_lon:high_lon]
                for i in range(group):
                    part = smoothed[t * block + i * depth:t * block + (i + 1) * depth]
                    summed = summed + (
                        pert[c * group + i, slot, :, low_lon:high_lon].astype(F32)
                        * part[:, :high_lon - low_lon]
                    )
                total[slot, :, low_lon:high_lon] = summed

    relay(0)

    def step(c, carry):
        relay(c + 1)
        process(c)
        return carry

    lax.fori_loop(0, chunks - 1, step, 0)
    process(chunks - 1)

    for level in range(levels):
        for slot in range(slots):
            levelled[slot, level] = total[slot, level * rows:(level + 1) * rows, :]

    def total_copy(k):
        return pltpu.make_async_remote_copy(
            src_ref=give.at[k - 1], dst_ref=take.at[k - 1],
            send_sem=t_send.at[k - 1], recv_sem=t_recv.at[k - 1],
            device_id=(lax.rem(me + k, holders), here), device_id_type=MESH,
        )

    for k in range(1, holders):
        holder = lax.rem(me + k, holders)
        for r in range(held_levels):
            level = owner[holder * held_levels + r]
            for slot in range(slots):
                give[k - 1, slot, r] = levelled[slot, level]
        total_copy(k).start()

    def drain(c, carry):
        own_copy(c).wait_send()

        @pl.when(has_target)
        def _():
            relay_copy(c).wait_send()

        return carry

    lax.fori_loop(0, chunks, drain, 0)
    for k in range(1, holders):
        total_copy(k).wait()
    for r in range(held_levels):
        level = owner[me * held_levels + r]
        for slot in range(slots):
            value = levelled[slot, level]
            for k in range(1, holders):
                value = value + take[k - 1, slot, r]
            out[slot, r] = value


def local(group, perturbations, gradient_held, block_owner):
    members, slots, levels, rows, lon = perturbations.shape
    held_levels = gradient_held.shape[1]
    holders = lax.axis_size("mem")
    depth = levels * rows
    chunks = members // group
    others = max(holders - 1, 1)
    wlat = jnp.asarray(level_row_weights(levels, rows, group))
    vmem = pl.BlockSpec(memory_space=pltpu.VMEM)
    part = (slots, held_levels, rows, lon)
    dma = pltpu.SemaphoreType.DMA
    return pl.pallas_call(
        functools.partial(kernel, group),
        out_shape=jax.ShapeDtypeStruct(part, F32),
        in_specs=[pl.BlockSpec(memory_space=pltpu.SMEM)] + [vmem] * 3,
        out_specs=vmem,
        scratch_shapes=[
            pltpu.VMEM((2, TILE + 2 * EDGE, TILE), BF16),
            pltpu.VMEM((holders,) + part, F32),
            pltpu.VMEM((slots, depth, lon), F32),
            pltpu.VMEM((members, depth, lon), BF16),
            pltpu.VMEM((members, depth, lon), BF16),
            pltpu.VMEM((members, depth, lon), BF16),
            pltpu.VMEM((slots, depth, lon), F32),
            pltpu.VMEM((slots, levels, rows, lon), F32),
            pltpu.VMEM((others,) + part, F32),
            pltpu.VMEM((others,) + part, F32),
            dma((others,)), dma((others,)),
            dma((chunks,)), dma((chunks,)),
            dma((chunks,)), dma((chunks,)),
            dma((others,)), dma((others,)),
        ],
        compiler_params=pltpu.CompilerParams(
            collective_id=0, has_side_effects=True, vmem_limit_bytes=48 * 1024 * 1024
        ),
    )(
        block_owner,
        perturbations.reshape(members, slots, depth, lon),
        gradient_held, wlat,
    )


def solution(mesh):
    placed = (P("mem", None, None, "lat", None), P(None, "mem", "lat", None), P())
    return jax.shard_map(
        functools.partial(local, 2),
        mesh=mesh, in_specs=placed, out_specs=P(None, "mem", "lat", None), check_vma=False,
    )
```

time: 134 us -> 35.4 us (0.26)
  the two profiles are of different devices: /device:TPU:25 before, /device:TPU:3 now
where the time goes in v1:
time: 35.4 us; the launch traced here: 35.2 us
  Pallas kernels  31.7 us (90%)
  local copies, waits for them, and re-layouts  3.45 us (10%)
    pallas_call x1, Pallas kernels, local(): pl.pallas_call(functools.partial(kernel, group), out_shape=jax.ShapeDtype...  31.7 us
    reshape x1, local copies, waits for them, and re-layouts, local(): perturbations.reshape(members, slots, depth, lon)  2.8 us

profile of v1, /device:TPU:3, one launch (start us, length us, event | category | flops | bytes accessed | tf_op | source)
XLA Modules:
  0.0 35.2 jit_solution(18431371490958032336)
XLA Ops:
  0.0 0.0 copy-start.1
  0.0 0.0 copy-start.2
  0.0 0.0 copy-start
  0.0 2.8 %reshape.3.pert = bf16[16,2,16,1440]{3,2,1,0:T(8,128)(2,1)S(1)} reshape(bf16[16,2,4,4,1440]{4,3,2,1,0:T(4,128)(2,1)} %param.4) | data formatting | bytes 2949120 | tf_op jit(solution)/shard_map/reshape | solution.py:288
  2.8 0.0 copy-done.1
  2.8 0.0 copy-done.2
  2.8 0.0 copy-done
  2.8 31.7 %shard_map.46 = f32[2,2,4,1440]{3,2,1,0:T(4,128)S(1)} custom-call(s32[4]{0:T(128)S(1)} %copy-done.2, bf16[16,2,16,1440]{3,2,1,0:T(8,128)(2,1)S(1)} %reshape.3.pert, f32[2,2,4,1440]{3,2,1,0:T(4,128)S(1)} %copy-done, bf16[2,64,96]{2,1,0:T(8,128)(2,1)S(1)} %copy-done.1), custom_call_target="tpu_custom_call" | custom-call | tf_op jit(solution)/shard_map/pallas_call | solution.py:262
  34.5 0.6 %copy.6 = f32[2,2,4,1440]{3,2,1,0:T(4,128)} copy(f32[2,2,4,1440]{3,2,1,0:T(4,128)S(1)} %shard_map.46) | data formatting | bytes 184320
Async XLA Ops:
  0.0 2.8 %copy-start.1 = (bf16[2,64,96]{2,1,0:T(8,128)(2,1)S(1)}, bf16[2,64,96]{2,1,0:T(8,128)(2,1)}, u32[]{:S(2)}) copy-start(bf16[2,64,96]{2,1,0:T(8,128)(2,1)} %constant.2.clone.wlat) | copy-start | bytes 73732
  0.0 2.8 %copy-start.2 = (s32[4]{0:T(128)S(1)}, s32[4]{0:T(128)}, u32[]{:S(2)}) copy-start(s32[4]{0:T(128)} %owner.1) | copy-start | bytes 52
  0.0 2.8 %copy-start = (f32[2,2,4,1440]{3,2,1,0:T(4,128)S(1)}, f32[2,2,4,1440]{3,2,1,0:T(4,128)}, u32[]{:S(2)}) copy-start(f32[2,2,4,1440]{3,2,1,0:T(4,128)} %held.1) | copy-start | bytes 276484

commit v2 on v1

--- a/solution.py
+++ b/solution.py
@@ -58,9 +58,9 @@
 
 
 def kernel(
-    group, owner, pert, held, wlat, out,
-    wlon, gbuf, gord, cbuf, dbuf, rbuf, total, levelled, give, take,
-    g_send, g_recv, c_send, c_recv, f_send, f_recv, t_send, t_recv,
+    group, ahead, owner, fields, held, wlat, out,
+    raw, pert, wlon, gbuf, gord, cbuf, dbuf, rbuf, total, levelled, give, take,
+    p_sem, g_send, g_recv, c_send, c_recv, f_send, f_recv, t_send, t_recv,
 ):
     members, slots, depth, lon = pert.shape
     holders, _, held_levels, rows, _ = gbuf.shape
@@ -68,6 +68,15 @@
     chunks = members // group
     tiles = -(-lon // TILE)
     right_pad = tiles * TILE + EDGE - lon
+
+    def field_copy(m):
+        return pltpu.make_async_copy(fields.at[m], raw.at[m], p_sem.at[m])
+
+    def start_fields(m, carry):
+        field_copy(m).start()
+        return carry
+
+    lax.fori_loop(0, members, start_fields, 0)
 
     me = lax.axis_index("mem")
     here = lax.axis_index("lat")
@@ -95,6 +104,12 @@
     def _():
         pl.semaphore_signal(barrier, inc=1, device_id=(me, source), device_id_type=MESH)
 
+    fill_lon_weights(wlon)
+
+    @pl.when(jnp.logical_not(has_source))
+    def _():
+        rbuf[...] = jnp.zeros_like(rbuf)
+
     pl.semaphore_wait(barrier, holders + has_target.astype(jnp.int32) + has_source.astype(jnp.int32))
 
     def gradient_copy(k):
@@ -107,12 +122,6 @@
     for k in range(1, holders):
         gradient_copy(k).start()
     gbuf[me] = held[...]
-    fill_lon_weights(wlon)
-
-    @pl.when(jnp.logical_not(has_source))
-    def _():
-        rbuf[...] = jnp.zeros_like(rbuf)
-
     total[...] = jnp.zeros_like(total)
     for k in range(1, holders):
         gradient_copy(k).wait()
@@ -145,9 +154,15 @@
     def control_step(c, carry):
         for i in range(group):
             m = c * group + i
-            value = pert[m, 0].astype(F32) * gord[0]
-            for slot in range(1, slots):
-                value = value + pert[m, slot].astype(F32) * gord[slot]
+            field_copy(m).wait()
+            value = None
+            for slot in range(slots):
+                field = jnp.concatenate(
+                    [raw[m, slot, level].astype(F32) for level in range(levels)], axis=0
+                )
+                pert[m, slot] = field.astype(BF16)
+                term = field * gord[slot]
+                value = term if value is None else value + term
             cbuf[m] = value.astype(BF16)
         own_copy(c).start()
         return carry
@@ -198,15 +213,24 @@
                     )
                 total[slot, :, low_lon:high_lon] = summed
 
-    relay(0)
+    lead = min(ahead, chunks)
+
+    def relay_step(c, carry):
+        relay(c)
+        return carry
 
     def step(c, carry):
-        relay(c + 1)
+        relay(c + lead)
         process(c)
         return carry
 
-    lax.fori_loop(0, chunks - 1, step, 0)
-    process(chunks - 1)
+    def last_step(c, carry):
+        process(c)
+        return carry
+
+    lax.fori_loop(0, lead, relay_step, 0)
+    lax.fori_loop(0, chunks - lead, step, 0)
+    lax.fori_loop(chunks - lead, chunks, last_step, 0)
 
     for level in range(levels):
         for slot in range(slots):
@@ -248,7 +272,7 @@
             out[slot, r] = value
 
 
-def local(group, perturbations, gradient_held, block_owner):
+def local(group, ahead, perturbations, gradient_held, block_owner):
     members, slots, levels, rows, lon = perturbations.shape
     held_levels = gradient_held.shape[1]
     holders = lax.axis_size("mem")
@@ -260,11 +284,15 @@
     part = (slots, held_levels, rows, lon)
     dma = pltpu.SemaphoreType.DMA
     return pl.pallas_call(
-        functools.partial(kernel, group),
+        functools.partial(kernel, group, ahead),
         out_shape=jax.ShapeDtypeStruct(part, F32),
-        in_specs=[pl.BlockSpec(memory_space=pltpu.SMEM)] + [vmem] * 3,
+        in_specs=[
+            pl.BlockSpec(memory_space=pltpu.SMEM), pl.BlockSpec(memory_space=pltpu.HBM), vmem, vmem,
+        ],
         out_specs=vmem,
         scratch_shapes=[
+            pltpu.VMEM((members, slots, levels, rows, lon), BF16),
+            pltpu.VMEM((members, slots, depth, lon), BF16),
             pltpu.VMEM((2, TILE + 2 * EDGE, TILE), BF16),
             pltpu.VMEM((holders,) + part, F32),
             pltpu.VMEM((slots, depth, lon), F32),
@@ -275,24 +303,23 @@
             pltpu.VMEM((slots, levels, rows, lon), F32),
             pltpu.VMEM((others,) + part, F32),
             pltpu.VMEM((others,) + part, F32),
+            dma((members,)),
             dma((others,)), dma((others,)),
             dma((chunks,)), dma((chunks,)),
             dma((chunks,)), dma((chunks,)),
             dma((others,)), dma((others,)),
         ],
         compiler_params=pltpu.CompilerParams(
-            collective_id=0, has_side_effects=True, vmem_limit_bytes=48 * 1024 * 1024
+            collective_id=0, has_side_effects=True, vmem_limit_bytes=63 * 1024 * 1024
         ),
     )(
-        block_owner,
-        perturbations.reshape(members, slots, depth, lon),
-        gradient_held, wlat,
+        block_owner, perturbations, gradient_held, wlat,
     )
 
 
 def solution(mesh):
     placed = (P("mem", None, None, "lat", None), P(None, "mem", "lat", None), P())
     return jax.shard_map(
-        functools.partial(local, 2),
+        functools.partial(local, 1, 3),
         mesh=mesh, in_specs=placed, out_specs=P(None, "mem", "lat", None), check_vma=False,
     )

time: 35.4 us -> 31.8 us (0.90)
  the two profiles are of different devices: /device:TPU:3 before, /device:TPU:25 now
where the time goes in v2:
time: 31.8 us; the launch traced here: 31.6 us
  Pallas kernels  30 us (94%)
  local copies, waits for them, and re-layouts  1.54 us (5%)
    pallas_call x1, Pallas kernels, local(): pl.pallas_call(functools.partial(kernel, group, ahead), out_shape=jax.Sha...  30 us
    unnamed x1, local copies, waits for them, and re-layouts  1.54 us

profile of v2, /device:TPU:25, one launch (start us, length us, event | category | flops | bytes accessed | tf_op | source)
XLA Modules:
  0.0 31.6 jit_solution(16268819760895841463)
XLA Ops:
  0.0 30.0 %shard_map.46 = f32[2,2,4,1440]{3,2,1,0:T(4,128)} custom-call(s32[4]{0:T(128)} %owner.1, bf16[16,2,4,4,1440]{4,3,2,1,0:T(4,128)(2,1)} %fields.1, f32[2,2,4,1440]{3,2,1,0:T(4,128)} %held.1, bf16[2,32,48]{2,1,0:T(8,128)(2,1)} %constant.2.clone.wlat), custom_call_target="tpu_custom_call" | custom-call | tf_op jit(solution)/shard_map/pallas_call | solution.py:286
  30.0 1.5 %copy.6 = f32[2,2,4,1440]{3,2,1,0:T(4,128)} copy(f32[2,2,4,1440]{3,2,1,0:T(4,128)} %shard_map.46) | data formatting | bytes 184320

commit v3 on v2

v3 whole, which is shorter than its diff:
```python
import functools
import math

import jax
import jax.numpy as jnp
import ml_dtypes
import numpy as np
from jax import lax
from jax.experimental import pallas as pl
from jax.experimental.pallas import tpu as pltpu
from jax.sharding import PartitionSpec as P

MESH = pl.DeviceIdType.MESH
REACH = 4
LANES = 128
F32 = jnp.float32
BF16 = jnp.bfloat16


def rho(offset, spread):
    if abs(offset) > REACH:
        return 0.0
    return math.exp(-(offset * offset) / (2.0 * spread * spread))


def split_weights(exact):
    high = exact.astype(ml_dtypes.bfloat16)
    low = (exact - high.astype(np.float64)).astype(ml_dtypes.bfloat16)
    return high, low


def level_row_weights(levels, rows, group):
    lev = np.array([[rho(a - b, 2.0) for b in range(levels)] for a in range(levels)])

    def block(shift):
        lat = np.array([[rho(b + shift * rows - a, 2.5) for b in range(rows)] for a in range(rows)])
        return np.kron(np.eye(group), np.kron(lev, lat))

    both = []
    for direct in (1, -1):
        high, low = split_weights(np.concatenate([block(0), block(direct), block(-direct)], axis=1))
        both.append(np.concatenate([high, low], axis=0))
    return np.stack(both)


def kernel(
    group, ahead, owner, fields, held, wlat, out,
    raw, pert, gbuf, gord, cbuf, dbuf, rbuf, total, wide, levelled, give, take,
    p_sem, g_send, g_recv, c_send, c_recv, f_send, f_recv, t_send, t_recv,
):
    members, slots, depth, lon = pert.shape
    holders, _, held_levels, rows, _ = gbuf.shape
    levels = depth // rows
    width = -(-(lon + 2 * REACH) // LANES) * LANES
    after = (width - lon) // 2
    before = width - lon - after

    def field_copy(m):
        return pltpu.make_async_copy(fields.at[m], raw.at[m], p_sem.at[m])

    def start_fields(m, carry):
        field_copy(m).start()
        return carry

    lax.fori_loop(0, members, start_fields, 0)

    me = lax.axis_index("mem")
    here = lax.axis_index("lat")
    count = lax.axis_size("lat")
    parity = lax.rem(here, 2)
    partner = here + 1 - 2 * parity
    hop = 2 - 4 * parity
    target = here + hop
    source = here - hop
    has_target = jnp.logical_and(target >= 0, target < count)
    has_source = jnp.logical_and(source >= 0, source < count)

    barrier = pltpu.get_barrier_semaphore()
    for k in range(1, holders):
        pl.semaphore_signal(
            barrier, inc=1, device_id=(lax.rem(me + k, holders), here), device_id_type=MESH
        )
    pl.semaphore_signal(barrier, inc=1, device_id=(me, partner), device_id_type=MESH)

    @pl.when(has_target)
    def _():
        pl.semaphore_signal(barrier, inc=1, device_id=(me, target), device_id_type=MESH)

    @pl.when(has_source)
    def _():
        pl.semaphore_signal(barrier, inc=1, device_id=(me, source), device_id_type=MESH)

    @pl.when(jnp.logical_not(has_source))
    def _():
        rbuf[...] = jnp.zeros_like(rbuf)

    pl.semaphore_wait(barrier, holders + has_target.astype(jnp.int32) + has_source.astype(jnp.int32))

    def gradient_copy(k):
        return pltpu.make_async_remote_copy(
            src_ref=held, dst_ref=gbuf.at[me],
            send_sem=g_send.at[k - 1], recv_sem=g_recv.at[k - 1],
            device_id=(lax.rem(me + k, holders), here), device_id_type=MESH,
        )

    for k in range(1, holders):
        gradient_copy(k).start()
    gbuf[me] = held[...]
    total[...] = jnp.zeros_like(total)
    for k in range(1, holders):
        gradient_copy(k).wait()

    for level in range(levels):
        place = jnp.int32(0)
        for p in range(levels):
            place = jnp.where(owner[p] == level, p, place)
        holder = lax.div(place, held_levels)
        within = lax.rem(place, held_levels)
        for slot in range(slots):
            gord[slot, level * rows:(level + 1) * rows, :] = gbuf[holder, slot, within]

    def own_copy(m):
        return pltpu.make_async_remote_copy(
            src_ref=cbuf.at[m], dst_ref=dbuf.at[m],
            send_sem=c_send.at[m], recv_sem=c_recv.at[m],
            device_id=(me, partner), device_id_type=MESH,
        )

    def relay_copy(m):
        return pltpu.make_async_remote_copy(
            src_ref=dbuf.at[m], dst_ref=rbuf.at[m],
            send_sem=f_send.at[m], recv_sem=f_recv.at[m],
            device_id=(me, target), device_id_type=MESH,
        )

    def control_step(m, carry):
        field_copy(m).wait()
        value = None
        for slot in range(slots):
            field = jnp.concatenate(
                [raw[m, slot, level].astype(F32) for level in range(levels)], axis=0
            )
            pert[m, slot] = field.astype(BF16)
            term = field * gord[slot]
            value = term if value is None else value + term
        cbuf[m] = value.astype(BF16)
        own_copy(m).start()
        return carry

    lax.fori_loop(0, members, control_step, 0)

    def relay(m):
        own_copy(m).wait_recv()

        @pl.when(has_target)
        def _():
            relay_copy(m).start()

    def process(first):
        @pl.when(has_source)
        def _():
            for i in range(group):
                relay_copy(first + i).wait_recv()

        span = pl.ds(first, group)
        block = group * depth
        stack = jnp.concatenate(
            [buf[span].reshape(block, lon) for buf in (cbuf, dbuf, rbuf)], axis=0
        )
        mixed = jnp.dot(wlat[parity], stack, preferred_element_type=F32)
        mixed = mixed[:block] + mixed[block:]
        wide[...] = jnp.concatenate([mixed, mixed[:, :after], mixed[:, lon - before:]], axis=1)
        for i in range(group):
            ring = wide[i * depth:(i + 1) * depth, :]
            smoothed = rho(0, 3.0) * ring
            for k in range(1, REACH + 1):
                pair = pltpu.roll(ring, k, 1) + pltpu.roll(ring, width - k, 1)
                smoothed = smoothed + rho(k, 3.0) * pair
            smoothed = smoothed[:, :lon]
            for slot in range(slots):
                total[slot] += pert[first + i, slot].astype(F32) * smoothed

    groups = members // group
    lead = min(ahead, groups)

    def relay_group(g):
        for i in range(group):
            relay(g * group + i)

    def relay_step(g, carry):
        relay_group(g)
        return carry

    def step(g, carry):
        relay_group(g + lead)
        process(g * group)
        return carry

    def last_step(g, carry):
        process(g * group)
        return carry

    lax.fori_loop(0, lead, relay_step, 0)
    lax.fori_loop(0, groups - lead, step, 0)
    lax.fori_loop(groups - lead, groups, last_step, 0)

    for level in range(levels):
        for slot in range(slots):
            levelled[slot, level] = total[slot, level * rows:(level + 1) * rows, :]

    def total_copy(k):
        return pltpu.make_async_remote_copy(
            src_ref=give.at[k - 1], dst_ref=take.at[k - 1],
            send_sem=t_send.at[k - 1], recv_sem=t_recv.at[k - 1],
            device_id=(lax.rem(me + k, holders), here), device_id_type=MESH,
        )

    for k in range(1, holders):
        holder = lax.rem(me + k, holders)
        for r in range(held_levels):
            level = owner[holder * held_levels + r]
            for slot in range(slots):
                give[k - 1, slot, r] = levelled[slot, level]
        total_copy(k).start()

    def drain(m, carry):
        own_copy(m).wait_send()

        @pl.when(has_target)
        def _():
            relay_copy(m).wait_send()

        return carry

    lax.fori_loop(0, members, drain, 0)
    for k in range(1, holders):
        total_copy(k).wait()
    for r in range(held_levels):
        level = owner[me * held_levels + r]
        for slot in range(slots):
            value = levelled[slot, level]
            for k in range(1, holders):
                value = value + take[k - 1, slot, r]
            out[slot, r] = value


def local(group, ahead, perturbations, gradient_held, block_owner):
    members, slots, levels, rows, lon = perturbations.shape
    held_levels = gradient_held.shape[1]
    holders = lax.axis_size("mem")
    depth = levels * rows
    others = max(holders - 1, 1)
    width = -(-(lon + 2 * REACH) // LANES) * LANES
    wlat = jnp.asarray(level_row_weights(levels, rows, group))
    vmem = pl.BlockSpec(memory_space=pltpu.VMEM)
    part = (slots, held_levels, rows, lon)
    dma = pltpu.SemaphoreType.DMA
    return pl.pallas_call(
        functools.partial(kernel, group, ahead),
        out_shape=jax.ShapeDtypeStruct(part, F32),
        in_specs=[
            pl.BlockSpec(memory_space=pltpu.SMEM), pl.BlockSpec(memory_space=pltpu.HBM), vmem, vmem,
        ],
        out_specs=vmem,
        scratch_shapes=[
            pltpu.VMEM((members, slots, levels, rows, lon), BF16),
            pltpu.VMEM((members, slots, depth, lon), BF16),
            pltpu.VMEM((holders,) + part, F32),
            pltpu.VMEM((slots, depth, lon), F32),
            pltpu.VMEM((members, depth, lon), BF16),
            pltpu.VMEM((members, depth, lon), BF16),
            pltpu.VMEM((members, depth, lon), BF16),
            pltpu.VMEM((slots, depth, lon), F32),
            pltpu.VMEM((group * depth, width), F32),
            pltpu.VMEM((slots, levels, rows, lon), F32),
            pltpu.VMEM((others,) + part, F32),
            pltpu.VMEM((others,) + part, F32),
            dma((members,)),
            dma((others,)), dma((others,)),
            dma((members,)), dma((members,)),
            dma((members,)), dma((members,)),
            dma((others,)), dma((others,)),
        ],
        compiler_params=pltpu.CompilerParams(
            collective_id=0, has_side_effects=True, vmem_limit_bytes=56 * 1024 * 1024
        ),
    )(
        block_owner, perturbations, gradient_held, wlat,
    )


def solution(mesh):
    placed = (P("mem", None, None, "lat", None), P(None, "mem", "lat", None), P())
    return jax.shard_map(
        functools.partial(local, 2, 2),
        mesh=mesh, in_specs=placed, out_specs=P(None, "mem", "lat", None), check_vma=False,
    )
```

time: 31.8 us -> 32 us (level)
  no operation moved by 1% of the time
where the time goes in v3:
time: 32 us; the launch traced here: 31.8 us
  Pallas kernels  30.3 us (95%)
  local copies, waits for them, and re-layouts  1.54 us (5%)
    pallas_call x1, Pallas kernels, local(): pl.pallas_call(functools.partial(kernel, group, ahead), out_shape=jax.Sha...  30.3 us
    unnamed x1, local copies, waits for them, and re-layouts  1.54 us

profile of v3, /device:TPU:25, one launch (start us, length us, event | category | flops | bytes accessed | tf_op | source)
XLA Modules:
  0.0 31.8 jit_solution(11029574767053628512)
XLA Ops:
  0.0 30.3 %shard_map.46 = f32[2,2,4,1440]{3,2,1,0:T(4,128)} custom-call(s32[4]{0:T(128)} %owner.1, bf16[16,2,4,4,1440]{4,3,2,1,0:T(4,128)(2,1)} %fields.1, f32[2,2,4,1440]{3,2,1,0:T(4,128)} %held.1, bf16[2,64,96]{2,1,0:T(8,128)(2,1)} %constant.2.clone.wlat), custom_call_target="tpu_custom_call" | custom-call | tf_op jit(solution)/shard_map/pallas_call | solution.py:258
  30.3 1.5 %copy.6 = f32[2,2,4,1440]{3,2,1,0:T(4,128)} copy(f32[2,2,4,1440]{3,2,1,0:T(4,128)} %shard_map.46) | data formatting | bytes 184320

commit v4 on v3

--- a/solution.py
+++ b/solution.py
@@ -64,6 +64,20 @@
 
     lax.fori_loop(0, members, start_fields, 0)
 
+    groups = members // group
+    early = min(4, groups)
+
+    def convert(m):
+        field_copy(m).wait()
+        for slot in range(slots):
+            pert[m, slot] = jnp.concatenate(
+                [raw[m, slot, level].astype(F32) for level in range(levels)], axis=0
+            ).astype(BF16)
+
+    def convert_step(m, carry):
+        convert(m)
+        return carry
+
     me = lax.axis_index("mem")
     here = lax.axis_index("lat")
     count = lax.axis_size("lat")
@@ -94,6 +108,8 @@
     def _():
         rbuf[...] = jnp.zeros_like(rbuf)
 
+    half = early * group // 2
+    lax.fori_loop(0, half, convert_step, 0)
     pl.semaphore_wait(barrier, holders + has_target.astype(jnp.int32) + has_source.astype(jnp.int32))
 
     def gradient_copy(k):
@@ -107,6 +123,7 @@
         gradient_copy(k).start()
     gbuf[me] = held[...]
     total[...] = jnp.zeros_like(total)
+    lax.fori_loop(half, early * group, convert_step, 0)
     for k in range(1, holders):
         gradient_copy(k).wait()
 
@@ -133,21 +150,13 @@
             device_id=(me, target), device_id_type=MESH,
         )
 
-    def control_step(m, carry):
-        field_copy(m).wait()
+    def control(m):
         value = None
         for slot in range(slots):
-            field = jnp.concatenate(
-                [raw[m, slot, level].astype(F32) for level in range(levels)], axis=0
-            )
-            pert[m, slot] = field.astype(BF16)
-            term = field * gord[slot]
+            term = pert[m, slot].astype(F32) * gord[slot]
             value = term if value is None else value + term
         cbuf[m] = value.astype(BF16)
         own_copy(m).start()
-        return carry
-
-    lax.fori_loop(0, members, control_step, 0)
 
     def relay(m):
         own_copy(m).wait_recv()
@@ -180,29 +189,29 @@
             for slot in range(slots):
                 total[slot] += pert[first + i, slot].astype(F32) * smoothed
 
-    groups = members // group
-    lead = min(ahead, groups)
-
-    def relay_group(g):
-        for i in range(group):
-            relay(g * group + i)
-
-    def relay_step(g, carry):
-        relay_group(g)
-        return carry
-
-    def step(g, carry):
-        relay_group(g + lead)
-        process(g * group)
-        return carry
-
-    def last_step(g, carry):
-        process(g * group)
-        return carry
-
-    lax.fori_loop(0, lead, relay_step, 0)
-    lax.fori_loop(0, groups - lead, step, 0)
-    lax.fori_loop(groups - lead, groups, last_step, 0)
+    def stage(first, last, convert_on, control_on, relay_on, process_on):
+        def step(g, carry):
+            for i in range(group):
+                if control_on:
+                    control(g * group + i)
+                if convert_on:
+                    convert((g + early) * group + i)
+            for i in range(group):
+                if relay_on:
+                    relay((g - ahead) * group + i)
+            if process_on:
+                process((g - 2 * ahead) * group)
+            return carry
+
+        if first < last:
+            lax.fori_loop(first, last, step, 0)
+
+    bounds = sorted({0, ahead, 2 * ahead, groups - early, groups, groups + ahead, groups + 2 * ahead})
+    for first, last in zip(bounds[:-1], bounds[1:]):
+        stage(
+            first, last, first < groups - early, first < groups,
+            ahead <= first < groups + ahead, 2 * ahead <= first,
+        )
 
     for level in range(levels):
         for slot in range(slots):
@@ -282,7 +291,7 @@
             dma((others,)), dma((others,)),
         ],
         compiler_params=pltpu.CompilerParams(
-            collective_id=0, has_side_effects=True, vmem_limit_bytes=56 * 1024 * 1024
+            collective_id=0, has_side_effects=True, vmem_limit_bytes=53 * 1024 * 1024
         ),
     )(
         block_owner, perturbations, gradient_held, wlat,

time: 32 us -> 32.5 us (1.016)
  local copies, waits for them, and re-layouts: 1.54 us -> 2.95 us
  Pallas kernels: 30.3 us -> 29.3 us
    unnamed x1 -> x7, local copies, waits for them, and re-layouts: 1.54 us -> 2.95 us
    pallas_call x1, Pallas kernels: 30.3 us -> 29.3 us  [local(): pl.pallas_call(functools.partial(kernel, group, ahead), out_shape=jax.Sha...]
where the time goes in v4:
time: 32.5 us; the launch traced here: 32.2 us
  Pallas kernels  29.3 us (90%)
  local copies, waits for them, and re-layouts  2.95 us (9%)
    pallas_call x1, Pallas kernels, local(): pl.pallas_call(functools.partial(kernel, group, ahead), out_shape=jax.Sha...  29.3 us
    unnamed x7, local copies, waits for them, and re-layouts  2.95 us

profile of v4, /device:TPU:25, one launch (start us, length us, event | category | flops | bytes accessed | tf_op | source)
XLA Modules:
  0.0 32.2 jit_solution(11538855165468471031)
XLA Ops:
  0.0 0.0 copy-start
  0.0 0.9 %copy-done = f32[2,2,4,1440]{3,2,1,0:T(4,128)S(1)} copy-done((f32[2,2,4,1440]{3,2,1,0:T(4,128)S(1)}, f32[2,2,4,1440]{3,2,1,0:T(4,128)}, u32[]{:S(2)}) %copy-start) | copy-done | bytes 92184
  0.9 0.0 copy-start.1
  0.9 0.8 %copy-done.1 = bf16[2,64,96]{2,1,0:T(8,128)(2,1)S(1)} copy-done((bf16[2,64,96]{2,1,0:T(8,128)(2,1)S(1)}, bf16[2,64,96]{2,1,0:T(8,128)(2,1)}, u32[]{:S(2)}) %copy-start.1) | copy-done | bytes 24600
  1.7 0.0 copy-start.2
  1.7 0.7 %copy-done.2 = s32[4]{0:T(128)S(1)} copy-done((s32[4]{0:T(128)S(1)}, s32[4]{0:T(128)}, u32[]{:S(2)}) %copy-start.2) | copy-done | bytes 40
  2.3 29.3 %shard_map.46 = f32[2,2,4,1440]{3,2,1,0:T(4,128)S(1)} custom-call(s32[4]{0:T(128)S(1)} %copy-done.2, bf16[16,2,4,4,1440]{4,3,2,1,0:T(4,128)(2,1)} %fields.1, f32[2,2,4,1440]{3,2,1,0:T(4,128)S(1)} %copy-done, bf16[2,64,96]{2,1,0:T(8,128)(2,1)S(1)} %copy-done.1), custom_call_target="tpu_custom_call" | custom-call | tf_op jit(solution)/shard_map/pallas_call | solution.py:267
  31.6 0.6 %copy.6 = f32[2,2,4,1440]{3,2,1,0:T(4,128)} copy(f32[2,2,4,1440]{3,2,1,0:T(4,128)S(1)} %shard_map.46) | data formatting | bytes 184320
Async XLA Ops:
  0.0 0.9 %copy-start = (f32[2,2,4,1440]{3,2,1,0:T(4,128)S(1)}, f32[2,2,4,1440]{3,2,1,0:T(4,128)}, u32[]{:S(2)}) copy-start(f32[2,2,4,1440]{3,2,1,0:T(4,128)} %held.1) | copy-start | bytes 276484
  0.9 0.8 %copy-start.1 = (bf16[2,64,96]{2,1,0:T(8,128)(2,1)S(1)}, bf16[2,64,96]{2,1,0:T(8,128)(2,1)}, u32[]{:S(2)}) copy-start(bf16[2,64,96]{2,1,0:T(8,128)(2,1)} %constant.2.clone.wlat) | copy-start | bytes 73732
  1.7 0.7 %copy-start.2 = (s32[4]{0:T(128)S(1)}, s32[4]{0:T(128)}, u32[]{:S(2)}) copy-start(s32[4]{0:T(128)} %owner.1) | copy-start | bytes 52

commit v5 on v4

v5 whole, which is shorter than its diff:
```python
import functools
import math

import jax
import jax.numpy as jnp
from jax import lax
from jax.experimental import pallas as pl
from jax.experimental.pallas import tpu as pltpu
from jax.sharding import PartitionSpec as P

MESH = pl.DeviceIdType.MESH
REACH = 4
LANES = 128
PAIR = 2
AHEAD = 2
F32 = jnp.float32
BF16 = jnp.bfloat16


def rho(offset, spread):
    return math.exp(-(offset * offset) / (2.0 * spread * spread))


def rho_of(apart, spread):
    value = jnp.zeros(apart.shape, F32)
    for a in range(REACH + 1):
        value = jnp.where(jnp.abs(apart) == a, rho(a, spread), value)
    return value


def fill_mixing(weights, owner, holders, held_levels, rows, direct):
    inner = PAIR * held_levels * rows
    block = holders * inner

    def places(axis):
        index = lax.broadcasted_iota(jnp.int32, (block, 3 * block), axis)
        part = jnp.where(index >= block, 1, 0) + jnp.where(index >= 2 * block, 1, 0)
        index = index - part * block
        level = jnp.zeros_like(index)
        member = jnp.zeros_like(index)
        row = index
        for p in range(holders * held_levels):
            for i in range(PAIR):
                start = (p // held_levels) * inner + (i * held_levels + p % held_levels) * rows
                inside = jnp.logical_and(index >= start, index < start + rows)
                level = jnp.where(inside, owner[p], level)
                member = jnp.where(inside, i, member)
                row = jnp.where(inside, index - start, row)
        shift = jnp.where(part == 1, direct, jnp.where(part == 2, -direct, 0))
        return level, member, row + shift * rows

    to_level, to_member, to_row = places(0)
    from_level, from_member, from_row = places(1)
    exact = rho_of(from_level - to_level, 2.0) * rho_of(from_row - to_row, 2.5)
    exact = jnp.where(from_member == to_member, exact, 0.0)
    high = exact.astype(BF16)
    weights[:block, :] = high
    weights[block:, :] = (exact - high.astype(F32)).astype(BF16)


def kernel(
    owner, fields, held, out,
    raw, pert, gbuf, grad, cbuf, dbuf, rbuf, weights, wide, total, give, take,
    p_sem, g_send, g_recv, c_send, c_recv, f_send, f_recv, t_send, t_recv,
):
    members, slots, levels, rows, lon = fields.shape
    held_levels = held.shape[1]
    holders = levels // held_levels
    pairs = members // PAIR
    inner = PAIR * held_levels * rows
    block = holders * inner
    half = held_levels * rows
    width = wide.shape[1]
    after = (width - lon) // 2
    before = width - lon - after
    early = min(AHEAD, pairs)

    fetch = pltpu.make_async_copy(fields, raw, p_sem.at[0])
    fetch.start()

    me = lax.axis_index("mem")
    here = lax.axis_index("lat")
    count = lax.axis_size("lat")
    parity = lax.rem(here, 2)
    partner = here + 1 - 2 * parity
    hop = 2 - 4 * parity
    target = here + hop
    source = here - hop
    has_target = jnp.logical_and(target >= 0, target < count)
    has_source = jnp.logical_and(source >= 0, source < count)

    barrier = pltpu.get_barrier_semaphore()
    for k in range(1, holders):
        pl.semaphore_signal(
            barrier, inc=1, device_id=(lax.rem(me + k, holders), here), device_id_type=MESH
        )
    pl.semaphore_signal(barrier, inc=1, device_id=(me, partner), device_id_type=MESH)

    @pl.when(has_target)
    def _():
        pl.semaphore_signal(barrier, inc=1, device_id=(me, target), device_id_type=MESH)

    @pl.when(has_source)
    def _():
        pl.semaphore_signal(barrier, inc=1, device_id=(me, source), device_id_type=MESH)

    def gradient_copy(k):
        return pltpu.make_async_remote_copy(
            src_ref=held, dst_ref=gbuf.at[me],
            send_sem=g_send.at[k - 1], recv_sem=g_recv.at[k - 1],
            device_id=(lax.rem(me + k, holders), here), device_id_type=MESH,
        )

    def own_copy(g, holder):
        return pltpu.make_async_remote_copy(
            src_ref=cbuf.at[g, holder], dst_ref=dbuf.at[g, holder],
            send_sem=c_send.at[g, holder], recv_sem=c_recv.at[g, holder],
            device_id=(me, partner), device_id_type=MESH,
        )

    def relay_copy(g, holder):
        return pltpu.make_async_remote_copy(
            src_ref=dbuf.at[g, holder], dst_ref=rbuf.at[g, holder],
            send_sem=f_send.at[g, holder], recv_sem=f_recv.at[g, holder],
            device_id=(me, target), device_id_type=MESH,
        )

    def convert(g, carry=0):
        for slot in range(slots):
            for holder in range(holders):
                pieces = [
                    raw[g * PAIR + i, slot, owner[holder * held_levels + r]].astype(F32)
                    for i in range(PAIR) for r in range(held_levels)
                ]
                pert[g, slot, holder] = jnp.concatenate(pieces, axis=0).astype(BF16)
        return carry

    def place_gradient(holder, block_ref):
        for slot in range(slots):
            pieces = [block_ref[slot, r] for r in range(held_levels)] * PAIR
            grad[slot, holder] = jnp.concatenate(pieces, axis=0)

    def control(g, holder):
        value = None
        for slot in range(slots):
            term = pert[g, slot, holder].astype(F32) * grad[slot, holder]
            value = term if value is None else value + term
        cbuf[g, holder] = value.astype(BF16)

    place_gradient(me, held)
    fetch.wait()
    for g in range(early):
        convert(g)
        control(g, me)

    pl.semaphore_wait(barrier, holders + has_target.astype(jnp.int32) + has_source.astype(jnp.int32))
    for k in range(1, holders):
        gradient_copy(k).start()
    for g in range(early):
        own_copy(g, me).start()

    @pl.when(jnp.logical_not(has_source))
    def _():
        rbuf[...] = jnp.zeros_like(rbuf)

    for k in range(1, holders):
        gradient_copy(k).wait_recv()
        holder = lax.rem(me + holders - k, holders)
        place_gradient(holder, gbuf.at[holder])

    for g in range(early):
        for k in range(1, holders):
            holder = lax.rem(me + k, holders)
            control(g, holder)
            own_copy(g, holder).start()

    total[...] = jnp.zeros_like(total)

    def send(g):
        convert(g)
        for k in range(holders):
            holder = lax.rem(me + k, holders)
            control(g, holder)
            own_copy(g, holder).start()

    def relay(g):
        for k in range(holders):
            holder = lax.rem(me + k, holders)
            own_copy(g, holder).wait_recv()

            @pl.when(has_target)
            def _():
                relay_copy(g, holder).start()

    def process(g):
        @pl.when(has_source)
        def _():
            for holder in range(holders):
                relay_copy(g, holder).wait_recv()

        stack = jnp.concatenate(
            [buf[g].reshape(block, lon) for buf in (cbuf, dbuf, rbuf)], axis=0
        )
        mixed = jnp.dot(weights[...], stack, preferred_element_type=F32)
        mixed = mixed[:block] + mixed[block:]
        wide[...] = jnp.concatenate([mixed, mixed[:, :after], mixed[:, lon - before:]], axis=1)
        for holder in range(holders):
            ring = wide[holder * inner:(holder + 1) * inner, :]
            smoothed = rho(0, 3.0) * ring
            for k in range(1, REACH + 1):
                both = pltpu.roll(ring, k, 1) + pltpu.roll(ring, width - k, 1)
                smoothed = smoothed + rho(k, 3.0) * both
            smoothed = smoothed[:, :lon]
            for slot in range(slots):
                total[slot, holder] += pert[g, slot, holder].astype(F32) * smoothed

    def stage(first, last, send_on, relay_on, process_on):
        def step(g, carry):
            if send_on:
                send(g)
            if relay_on:
                relay(g - AHEAD)
            if process_on:
                process(g - 2 * AHEAD)
            return carry

        if first < last:
            lax.fori_loop(first, last, step, 0)

    stage(early, early + 1, True, False, False)
    fill_mixing(weights, owner, holders, held_levels, rows, 1 - 2 * parity)
    relay(0)
    stage(early + 1, 2 * AHEAD, True, True, False)
    stage(2 * AHEAD, pairs, True, True, True)
    stage(pairs, pairs + AHEAD, False, True, True)
    stage(pairs + AHEAD, pairs + 2 * AHEAD, False, False, True)

    def total_copy(k):
        return pltpu.make_async_remote_copy(
            src_ref=give.at[k - 1], dst_ref=take.at[k - 1],
            send_sem=t_send.at[k - 1], recv_sem=t_recv.at[k - 1],
            device_id=(lax.rem(me + k, holders), here), device_id_type=MESH,
        )

    for k in range(1, holders):
        holder = lax.rem(me + k, holders)
        for slot in range(slots):
            full = total[slot, holder]
            give[k - 1, slot] = sum(full[i * half:(i + 1) * half] for i in range(1, PAIR)) + full[:half]
        total_copy(k).start()

    for k in range(1, holders):
        gradient_copy(k).wait_send()

    def drain(g, carry):
        for holder in range(holders):
            own_copy(g, holder).wait_send()

            @pl.when(has_target)
            def _():
                relay_copy(g, holder).wait_send()

        return carry

    lax.fori_loop(0, pairs, drain, 0)
    for k in range(1, holders):
        total_copy(k).wait()
    for slot in range(slots):
        full = total[slot, me]
        value = sum(full[i * half:(i + 1) * half] for i in range(1, PAIR)) + full[:half]
        for k in range(1, holders):
            value = value + take[k - 1, slot]
        for r in range(held_levels):
            out[slot, r] = value[r * rows:(r + 1) * rows]


def local(perturbations, gradient_held, block_owner):
    members, slots, levels, rows, lon = perturbations.shape
    held_levels = gradient_held.shape[1]
    holders = levels // held_levels
    pairs = members // PAIR
    inner = PAIR * held_levels * rows
    block = holders * inner
    others = max(holders - 1, 1)
    width = -(-(lon + 2 * REACH) // LANES) * LANES
    part = (slots, held_levels, rows, lon)
    dma = pltpu.SemaphoreType.DMA
    return pl.pallas_call(
        kernel,
        out_shape=jax.ShapeDtypeStruct(part, F32),
        in_specs=[
            pl.BlockSpec(memory_space=pltpu.SMEM),
            pl.BlockSpec(memory_space=pltpu.HBM),
            pl.BlockSpec(memory_space=pltpu.VMEM),
        ],
        out_specs=pl.BlockSpec(memory_space=pltpu.VMEM),
        scratch_shapes=[
            pltpu.VMEM((members, slots, levels, rows, lon), BF16),
            pltpu.VMEM((pairs, slots, holders, inner, lon), BF16),
            pltpu.VMEM((holders,) + part, F32),
            pltpu.VMEM((slots, holders, inner, lon), F32),
            pltpu.VMEM((pairs, holders, inner, lon), BF16),
            pltpu.VMEM((pairs, holders, inner, lon), BF16),
            pltpu.VMEM((pairs, holders, inner, lon), BF16),
            pltpu.VMEM((2 * block, 3 * block), BF16),
            pltpu.VMEM((block, width), F32),
            pltpu.VMEM((slots, holders, inner, lon), F32),
            pltpu.VMEM((others, slots, held_levels * rows, lon), F32),
            pltpu.VMEM((others, slots, held_levels * rows, lon), F32),
            dma((1,)),
            dma((others,)), dma((others,)),
            dma((pairs, holders)), dma((pairs, holders)),
            dma((pairs, holders)), dma((pairs, holders)),
            dma((others,)), dma((others,)),
        ],
        compiler_params=pltpu.CompilerParams(
            collective_id=0, has_side_effects=True, vmem_limit_bytes=538 * 1024 * 1024 // 10
        ),
    )(block_owner, perturbations, gradient_held)


def solution(mesh):
    placed = (P("mem", None, None, "lat", None), P(None, "mem", "lat", None), P())
    return jax.shard_map(
        local, mesh=mesh, in_specs=placed, out_specs=P(None, "mem", "lat", None), check_vma=False,
    )
```

time: 32.5 us -> 29.9 us (0.920)
  local copies, waits for them, and re-layouts: 2.95 us -> 1.3 us
  Pallas kernels: 29.3 us -> 28.4 us
    unnamed x7 -> x3, local copies, waits for them, and re-layouts: 2.95 us -> 1.3 us
    pallas_call x1, Pallas kernels: 29.3 us -> 28.4 us  [local(): pl.pallas_call(kernel, out_shape=jax.ShapeDtypeStruct(part, F32), in_spec...]
where the time goes in v5:
time: 29.9 us; the launch traced here: 29.7 us
  Pallas kernels  28.4 us (95%)
  local copies, waits for them, and re-layouts  1.3 us (4%)
    pallas_call x1, Pallas kernels, local(): pl.pallas_call(kernel, out_shape=jax.ShapeDtypeStruct(part, F32), in_spec...  28.4 us
    unnamed x3, local copies, waits for them, and re-layouts  1.3 us

profile of v5, /device:TPU:25, one launch (start us, length us, event | category | flops | bytes accessed | tf_op | source)
XLA Modules:
  0.0 29.7 jit_solution(17578104783858018771)
XLA Ops:
  0.0 0.0 copy-start
  0.0 0.7 %copy-done = s32[4]{0:T(128)S(1)} copy-done((s32[4]{0:T(128)S(1)}, s32[4]{0:T(128)}, u32[]{:S(2)}) %copy-start) | copy-done | bytes 40
  0.7 28.4 %shard_map.37 = f32[2,2,4,1440]{3,2,1,0:T(4,128)S(1)} custom-call(s32[4]{0:T(128)S(1)} %copy-done, bf16[16,2,4,4,1440]{4,3,2,1,0:T(4,128)(2,1)} %fields.1, f32[2,2,4,1440]{3,2,1,0:T(4,128)} %held.1), custom_call_target="tpu_custom_call" | custom-call | tf_op jit(solution)/shard_map/pallas_call | solution.py:288
  29.1 0.6 %copy.5 = f32[2,2,4,1440]{3,2,1,0:T(4,128)} copy(f32[2,2,4,1440]{3,2,1,0:T(4,128)S(1)} %shard_map.37) | data formatting | bytes 184320
Async XLA Ops:
  0.0 0.7 %copy-start = (s32[4]{0:T(128)S(1)}, s32[4]{0:T(128)}, u32[]{:S(2)}) copy-start(s32[4]{0:T(128)} %owner.1) | copy-start | bytes 52

commit v6 on v5

--- a/solution.py
+++ b/solution.py
@@ -60,8 +60,9 @@
 
 def kernel(
     owner, fields, held, out,
-    raw, pert, gbuf, grad, cbuf, dbuf, rbuf, weights, wide, total, give, take,
-    p_sem, g_send, g_recv, c_send, c_recv, f_send, f_recv, t_send, t_recv,
+    raw, pert, gbuf, grad, cbuf, dbuf, rbuf, ctail, dtail, rtail, weights, last, wide, total, give, take,
+    p_sem, g_send, g_recv, c_send, c_recv, f_send, f_recv,
+    ct_send, ct_recv, ft_send, ft_recv, t_send, t_recv,
 ):
     members, slots, levels, rows, lon = fields.shape
     held_levels = held.shape[1]
@@ -71,8 +72,12 @@
     block = holders * inner
     half = held_levels * rows
     width = wide.shape[1]
+    main = cbuf.shape[-1]
+    rest = lon - main
+    share = LANES // rest
+    quads = pairs // share
     after = (width - lon) // 2
-    before = width - lon - after
+    before = width - lon - after - rest
     early = min(AHEAD, pairs)
 
     fetch = pltpu.make_async_copy(fields, raw, p_sem.at[0])
@@ -125,6 +130,20 @@
             device_id=(me, target), device_id_type=MESH,
         )
 
+    def own_tail(q, holder):
+        return pltpu.make_async_remote_copy(
+            src_ref=ctail.at[q, holder], dst_ref=dtail.at[q, holder],
+            send_sem=ct_send.at[q, holder], recv_sem=ct_recv.at[q, holder],
+            device_id=(me, partner), device_id_type=MESH,
+        )
+
+    def relay_tail(q, holder):
+        return pltpu.make_async_remote_copy(
+            src_ref=dtail.at[q, holder], dst_ref=rtail.at[q, holder],
+            send_sem=ft_send.at[q, holder], recv_sem=ft_recv.at[q, holder],
+            device_id=(me, target), device_id_type=MESH,
+        )
+
     def convert(g, carry=0):
         for slot in range(slots):
             for holder in range(holders):
@@ -140,28 +159,33 @@
             pieces = [block_ref[slot, r] for r in range(held_levels)] * PAIR
             grad[slot, holder] = jnp.concatenate(pieces, axis=0)
 
-    def control(g, holder):
+    def product(g, holder, lanes):
         value = None
         for slot in range(slots):
-            term = pert[g, slot, holder].astype(F32) * grad[slot, holder]
+            term = pert[g, slot, holder, :, lanes].astype(F32) * grad[slot, holder, :, lanes]
             value = term if value is None else value + term
-        cbuf[g, holder] = value.astype(BF16)
+        return value
+
+    def control(g, holder):
+        cbuf[g, holder] = product(g, holder, slice(0, main)).astype(BF16)
 
     place_gradient(me, held)
     fetch.wait()
-    for g in range(early):
+    convert(0)
+    control(0, me)
+    pl.semaphore_wait(barrier, holders + has_target.astype(jnp.int32) + has_source.astype(jnp.int32))
+    for k in range(1, holders):
+        gradient_copy(k).start()
+    own_copy(0, me).start()
+    for g in range(1, early):
         convert(g)
         control(g, me)
-
-    pl.semaphore_wait(barrier, holders + has_target.astype(jnp.int32) + has_source.astype(jnp.int32))
-    for k in range(1, holders):
-        gradient_copy(k).start()
-    for g in range(early):
         own_copy(g, me).start()
 
     @pl.when(jnp.logical_not(has_source))
     def _():
         rbuf[...] = jnp.zeros_like(rbuf)
+        rtail[...] = jnp.zeros_like(rtail)
 
     for k in range(1, holders):
         gradient_copy(k).wait_recv()
@@ -176,8 +200,14 @@
 
     total[...] = jnp.zeros_like(total)
 
+    lax.fori_loop(early, pairs, convert, 0)
+    for q in range(quads):
+        for holder in range(holders):
+            tails = [product(q * share + j, holder, slice(main, lon)) for j in range(share)]
+            ctail[q, holder] = jnp.concatenate(tails, axis=1).astype(BF16)
+            own_tail(q, holder).start()
+
     def send(g):
-        convert(g)
         for k in range(holders):
             holder = lax.rem(me + k, holders)
             control(g, holder)
@@ -191,6 +221,25 @@
             @pl.when(has_target)
             def _():
                 relay_copy(g, holder).start()
+
+    def mix(stack):
+        mixed = jnp.dot(weights[...], stack, preferred_element_type=F32)
+        return mixed[:block] + mixed[block:]
+
+    def mix_tails():
+        @pl.when(has_source)
+        def _():
+            for q in range(quads):
+                for holder in range(holders):
+                    relay_tail(q, holder).wait_recv()
+
+        for q in range(quads):
+            stack = jnp.concatenate(
+                [buf[q].reshape(block, LANES) for buf in (ctail, dtail, rtail)], axis=0
+            )
+            mixed = mix(stack)
+            for j in range(share):
+                last[q * share + j] = mixed[:, j * rest:(j + 1) * rest]
 
     def process(g):
         @pl.when(has_source)
@@ -199,11 +248,14 @@
                 relay_copy(g, holder).wait_recv()
 
         stack = jnp.concatenate(
-            [buf[g].reshape(block, lon) for buf in (cbuf, dbuf, rbuf)], axis=0
-        )
-        mixed = jnp.dot(weights[...], stack, preferred_element_type=F32)
-        mixed = mixed[:block] + mixed[block:]
-        wide[...] = jnp.concatenate([mixed, mixed[:, :after], mixed[:, lon - before:]], axis=1)
+            [buf[g].reshape(block, main) for buf in (cbuf, dbuf, rbuf)], axis=0
+        )
+        mixed = mix(stack)
+        wide[:, :main] = mixed
+        tail = last[g]
+        wide[:, main:] = jnp.concatenate(
+            [tail, mixed[:, :after], mixed[:, main - before:], tail], axis=1
+        )
         for holder in range(holders):
             ring = wide[holder * inner:(holder + 1) * inner, :]
             smoothed = rho(0, 3.0) * ring
@@ -231,7 +283,18 @@
     fill_mixing(weights, owner, holders, held_levels, rows, 1 - 2 * parity)
     relay(0)
     stage(early + 1, 2 * AHEAD, True, True, False)
-    stage(2 * AHEAD, pairs, True, True, True)
+    for q in range(quads):
+        for holder in range(holders):
+            own_tail(q, holder).wait_recv()
+
+            @pl.when(has_target)
+            def _():
+                relay_tail(q, holder).start()
+
+    stage(2 * AHEAD, 2 * AHEAD + 1, True, True, False)
+    mix_tails()
+    process(0)
+    stage(2 * AHEAD + 1, pairs, True, True, True)
     stage(pairs, pairs + AHEAD, False, True, True)
     stage(pairs + AHEAD, pairs + 2 * AHEAD, False, False, True)
 
@@ -263,6 +326,14 @@
         return carry
 
     lax.fori_loop(0, pairs, drain, 0)
+    for q in range(quads):
+        for holder in range(holders):
+            own_tail(q, holder).wait_send()
+
+            @pl.when(has_target)
+            def _():
+                relay_tail(q, holder).wait_send()
+
     for k in range(1, holders):
         total_copy(k).wait()
     for slot in range(slots):
@@ -283,6 +354,10 @@
     block = holders * inner
     others = max(holders - 1, 1)
     width = -(-(lon + 2 * REACH) // LANES) * LANES
+    main = lon // LANES * LANES
+    rest = lon - main
+    share = LANES // rest
+    quads = pairs // share
     part = (slots, held_levels, rows, lon)
     dma = pltpu.SemaphoreType.DMA
     return pl.pallas_call(
@@ -299,10 +374,14 @@
             pltpu.VMEM((pairs, slots, holders, inner, lon), BF16),
             pltpu.VMEM((holders,) + part, F32),
             pltpu.VMEM((slots, holders, inner, lon), F32),
-            pltpu.VMEM((pairs, holders, inner, lon), BF16),
-            pltpu.VMEM((pairs, holders, inner, lon), BF16),
-            pltpu.VMEM((pairs, holders, inner, lon), BF16),
+            pltpu.VMEM((pairs, holders, inner, main), BF16),
+            pltpu.VMEM((pairs, holders, inner, main), BF16),
+            pltpu.VMEM((pairs, holders, inner, main), BF16),
+            pltpu.VMEM((quads, holders, inner, LANES), BF16),
+            pltpu.VMEM((quads, holders, inner, LANES), BF16),
+            pltpu.VMEM((quads, holders, inner, LANES), BF16),
             pltpu.VMEM((2 * block, 3 * block), BF16),
+            pltpu.VMEM((pairs, block, rest), F32),
             pltpu.VMEM((block, width), F32),
             pltpu.VMEM((slots, holders, inner, lon), F32),
             pltpu.VMEM((others, slots, held_levels * rows, lon), F32),
@@ -311,6 +390,8 @@
             dma((others,)), dma((others,)),
             dma((pairs, holders)), dma((pairs, holders)),
             dma((pairs, holders)), dma((pairs, holders)),
+            dma((quads, holders)), dma((quads, holders)),
+            dma((quads, holders)), dma((quads, holders)),
             dma((others,)), dma((others,)),
         ],
         compiler_params=pltpu.CompilerParams(

time: 29.9 us -> 29.7 us (level)
  Pallas kernels: 28.4 us -> 27.9 us
    pallas_call x1, Pallas kernels: 28.4 us -> 27.9 us  [local(): pl.pallas_call(kernel, out_shape=jax.ShapeDtypeStruct(part, F32), in_spec...]
where the time goes in v6:
time: 29.7 us; the launch traced here: 29.2 us
  Pallas kernels  27.9 us (94%)
  local copies, waits for them, and re-layouts  1.3 us (4%)
    pallas_call x1, Pallas kernels, local(): pl.pallas_call(kernel, out_shape=jax.ShapeDtypeStruct(part, F32), in_spec...  27.9 us
    unnamed x3, local copies, waits for them, and re-layouts  1.3 us

profile of v6, /device:TPU:25, one launch (start us, length us, event | category | flops | bytes accessed | tf_op | source)
XLA Modules:
  0.0 29.2 jit_solution(5803906927728507244)
XLA Ops:
  0.0 0.0 copy-start
  0.0 0.7 %copy-done = s32[4]{0:T(128)S(1)} copy-done((s32[4]{0:T(128)S(1)}, s32[4]{0:T(128)}, u32[]{:S(2)}) %copy-start) | copy-done | bytes 40
  0.7 27.9 %shard_map.37 = f32[2,2,4,1440]{3,2,1,0:T(4,128)S(1)} custom-call(s32[4]{0:T(128)S(1)} %copy-done, bf16[16,2,4,4,1440]{4,3,2,1,0:T(4,128)(2,1)} %fields.1, f32[2,2,4,1440]{3,2,1,0:T(4,128)} %held.1), custom_call_target="tpu_custom_call" | custom-call | tf_op jit(solution)/shard_map/pallas_call | solution.py:363
  28.6 0.6 %copy.5 = f32[2,2,4,1440]{3,2,1,0:T(4,128)} copy(f32[2,2,4,1440]{3,2,1,0:T(4,128)S(1)} %shard_map.37) | data formatting | bytes 184320
Async XLA Ops:
  0.0 0.7 %copy-start = (s32[4]{0:T(128)S(1)}, s32[4]{0:T(128)}, u32[]{:S(2)}) copy-start(s32[4]{0:T(128)} %owner.1) | copy-start | bytes 52

commit v7 on v6

--- a/solution.py
+++ b/solution.py
@@ -13,6 +13,7 @@
 LANES = 128
 PAIR = 2
 AHEAD = 2
+LAG = 3
 F32 = jnp.float32
 BF16 = jnp.bfloat16
 
@@ -273,7 +274,7 @@
             if relay_on:
                 relay(g - AHEAD)
             if process_on:
-                process(g - 2 * AHEAD)
+                process(g - AHEAD - LAG)
             return carry
 
         if first < last:
@@ -291,12 +292,12 @@
             def _():
                 relay_tail(q, holder).start()
 
-    stage(2 * AHEAD, 2 * AHEAD + 1, True, True, False)
+    stage(2 * AHEAD, AHEAD + LAG + 1, True, True, False)
     mix_tails()
     process(0)
-    stage(2 * AHEAD + 1, pairs, True, True, True)
+    stage(AHEAD + LAG + 1, pairs, True, True, True)
     stage(pairs, pairs + AHEAD, False, True, True)
-    stage(pairs + AHEAD, pairs + 2 * AHEAD, False, False, True)
+    stage(pairs + AHEAD, pairs + AHEAD + LAG, False, False, True)
 
     def total_copy(k):
         return pltpu.make_async_remote_copy(

time: 29.7 us -> 28.7 us (0.966)
  Pallas kernels: 27.9 us -> 27.2 us
    pallas_call x1, Pallas kernels: 27.9 us -> 27.2 us  [local(): pl.pallas_call(kernel, out_shape=jax.ShapeDtypeStruct(part, F32), in_spec...]
where the time goes in v7:
time: 28.7 us; the launch traced here: 28.5 us
  Pallas kernels  27.2 us (95%)
  local copies, waits for them, and re-layouts  1.3 us (5%)
    pallas_call x1, Pallas kernels, local(): pl.pallas_call(kernel, out_shape=jax.ShapeDtypeStruct(part, F32), in_spec...  27.2 us
    unnamed x3, local copies, waits for them, and re-layouts  1.3 us

profile of v7, /device:TPU:25, one launch (start us, length us, event | category | flops | bytes accessed | tf_op | source)
XLA Modules:
  0.0 28.5 jit_solution(12033816752608953748)
XLA Ops:
  0.0 0.0 copy-start
  0.0 0.7 %copy-done = s32[4]{0:T(128)S(1)} copy-done((s32[4]{0:T(128)S(1)}, s32[4]{0:T(128)}, u32[]{:S(2)}) %copy-start) | copy-done | bytes 40
  0.7 27.2 %shard_map.37 = f32[2,2,4,1440]{3,2,1,0:T(4,128)S(1)} custom-call(s32[4]{0:T(128)S(1)} %copy-done, bf16[16,2,4,4,1440]{4,3,2,1,0:T(4,128)(2,1)} %fields.1, f32[2,2,4,1440]{3,2,1,0:T(4,128)} %held.1), custom_call_target="tpu_custom_call" | custom-call | tf_op jit(solution)/shard_map/pallas_call | solution.py:364
  27.8 0.6 %copy.5 = f32[2,2,4,1440]{3,2,1,0:T(4,128)} copy(f32[2,2,4,1440]{3,2,1,0:T(4,128)S(1)} %shard_map.37) | data formatting | bytes 184320
Async XLA Ops:
  0.0 0.7 %copy-start = (s32[4]{0:T(128)S(1)}, s32[4]{0:T(128)}, u32[]{:S(2)}) copy-start(s32[4]{0:T(128)} %owner.1) | copy-start | bytes 52

commit v8 on v7

--- a/solution.py
+++ b/solution.py
@@ -60,8 +60,8 @@
 
 
 def kernel(
-    owner, fields, held, out,
-    raw, pert, gbuf, grad, cbuf, dbuf, rbuf, ctail, dtail, rtail, weights, last, wide, total, give, take,
+    owner, fields, held_far, out,
+    raw, raw_first, held, pert, gbuf, grad, cbuf, dbuf, rbuf, ctail, dtail, rtail, weights, last, wide, total, give, take,
     p_sem, g_send, g_recv, c_send, c_recv, f_send, f_recv,
     ct_send, ct_recv, ft_send, ft_recv, t_send, t_recv,
 ):
@@ -81,8 +81,9 @@
     before = width - lon - after - rest
     early = min(AHEAD, pairs)
 
-    fetch = pltpu.make_async_copy(fields, raw, p_sem.at[0])
-    fetch.start()
+    first_fetch = pltpu.make_async_copy(fields.at[pl.ds(0, PAIR)], raw_first, p_sem.at[0])
+    held_fetch = pltpu.make_async_copy(held_far, held, p_sem.at[1])
+    fetch = pltpu.make_async_copy(fields.at[pl.ds(PAIR, members - PAIR)], raw, p_sem.at[2])
 
     me = lax.axis_index("mem")
     here = lax.axis_index("lat")
@@ -110,6 +111,10 @@
     def _():
         pl.semaphore_signal(barrier, inc=1, device_id=(me, source), device_id_type=MESH)
 
+    held_fetch.start()
+    first_fetch.start()
+    fetch.start()
+
     def gradient_copy(k):
         return pltpu.make_async_remote_copy(
             src_ref=held, dst_ref=gbuf.at[me],
@@ -145,14 +150,17 @@
             device_id=(me, target), device_id_type=MESH,
         )
 
-    def convert(g, carry=0):
+    def convert_from(source, first, g):
         for slot in range(slots):
             for holder in range(holders):
                 pieces = [
-                    raw[g * PAIR + i, slot, owner[holder * held_levels + r]].astype(F32)
+                    source[first + i, slot, owner[holder * held_levels + r]].astype(F32)
                     for i in range(PAIR) for r in range(held_levels)
                 ]
                 pert[g, slot, holder] = jnp.concatenate(pieces, axis=0).astype(BF16)
+
+    def convert(g, carry=0):
+        convert_from(raw, (g - 1) * PAIR, g)
         return carry
 
     def place_gradient(holder, block_ref):
@@ -170,14 +178,16 @@
     def control(g, holder):
         cbuf[g, holder] = product(g, holder, slice(0, main)).astype(BF16)
 
+    held_fetch.wait()
     place_gradient(me, held)
-    fetch.wait()
-    convert(0)
+    first_fetch.wait()
+    convert_from(raw_first, 0, 0)
     control(0, me)
     pl.semaphore_wait(barrier, holders + has_target.astype(jnp.int32) + has_source.astype(jnp.int32))
     for k in range(1, holders):
         gradient_copy(k).start()
     own_copy(0, me).start()
+    fetch.wait()
     for g in range(1, early):
         convert(g)
         control(g, me)
@@ -367,11 +377,13 @@
         in_specs=[
             pl.BlockSpec(memory_space=pltpu.SMEM),
             pl.BlockSpec(memory_space=pltpu.HBM),
-            pl.BlockSpec(memory_space=pltpu.VMEM),
+            pl.BlockSpec(memory_space=pltpu.HBM),
         ],
         out_specs=pl.BlockSpec(memory_space=pltpu.VMEM),
         scratch_shapes=[
-            pltpu.VMEM((members, slots, levels, rows, lon), BF16),
+            pltpu.VMEM((members - PAIR, slots, levels, rows, lon), BF16),
+            pltpu.VMEM((PAIR, slots, levels, rows, lon), BF16),
+            pltpu.VMEM(part, F32),
             pltpu.VMEM((pairs, slots, holders, inner, lon), BF16),
             pltpu.VMEM((holders,) + part, F32),
             pltpu.VMEM((slots, holders, inner, lon), F32),
@@ -387,7 +399,7 @@
             pltpu.VMEM((slots, holders, inner, lon), F32),
             pltpu.VMEM((others, slots, held_levels * rows, lon), F32),
             pltpu.VMEM((others, slots, held_levels * rows, lon), F32),
-            dma((1,)),
+            dma((3,)),
             dma((others,)), dma((others,)),
             dma((pairs, holders)), dma((pairs, holders)),
             dma((pairs, holders)), dma((pairs, holders)),

time: 28.7 us -> 28.3 us (0.986)
  Pallas kernels: 27.2 us -> 26.8 us
    pallas_call x1, Pallas kernels: 27.2 us -> 26.8 us  [local(): pl.pallas_call(kernel, out_shape=jax.ShapeDtypeStruct(part, F32), in_spec...]
where the time goes in v8:
time: 28.3 us; the launch traced here: 28.1 us
  Pallas kernels  26.8 us (95%)
  local copies, waits for them, and re-layouts  1.3 us (5%)
    pallas_call x1, Pallas kernels, local(): pl.pallas_call(kernel, out_shape=jax.ShapeDtypeStruct(part, F32), in_spec...  26.8 us
    unnamed x3, local copies, waits for them, and re-layouts  1.3 us

profile of v8, /device:TPU:25, one launch (start us, length us, event | category | flops | bytes accessed | tf_op | source)
XLA Modules:
  0.0 28.1 jit_solution(5647614409596446157)
XLA Ops:
  0.0 0.0 copy-start
  0.0 0.7 %copy-done = s32[4]{0:T(128)S(1)} copy-done((s32[4]{0:T(128)S(1)}, s32[4]{0:T(128)}, u32[]{:S(2)}) %copy-start) | copy-done | bytes 40
  0.7 26.8 %shard_map.37 = f32[2,2,4,1440]{3,2,1,0:T(4,128)S(1)} custom-call(s32[4]{0:T(128)S(1)} %copy-done, bf16[16,2,4,4,1440]{4,3,2,1,0:T(4,128)(2,1)} %fields.1, f32[2,2,4,1440]{3,2,1,0:T(4,128)} %held_far.1), custom_call_target="tpu_custom_call" | custom-call | tf_op jit(solution)/shard_map/pallas_call | solution.py:374
  27.5 0.6 %copy.5 = f32[2,2,4,1440]{3,2,1,0:T(4,128)} copy(f32[2,2,4,1440]{3,2,1,0:T(4,128)S(1)} %shard_map.37) | data formatting | bytes 184320
Async XLA Ops:
  0.0 0.7 %copy-start = (s32[4]{0:T(128)S(1)}, s32[4]{0:T(128)}, u32[]{:S(2)}) copy-start(s32[4]{0:T(128)} %owner.1) | copy-start | bytes 52

commit v9 on v8

--- a/solution.py
+++ b/solution.py
@@ -209,14 +209,19 @@
             control(g, holder)
             own_copy(g, holder).start()
 
-    total[...] = jnp.zeros_like(total)
-
-    lax.fori_loop(early, pairs, convert, 0)
-    for q in range(quads):
+    def send_tails(q):
         for holder in range(holders):
             tails = [product(q * share + j, holder, slice(main, lon)) for j in range(share)]
             ctail[q, holder] = jnp.concatenate(tails, axis=1).astype(BF16)
             own_tail(q, holder).start()
+
+    def pass_tails(q):
+        for holder in range(holders):
+            own_tail(q, holder).wait_recv()
+
+            @pl.when(has_target)
+            def _():
+                relay_tail(q, holder).start()
 
     def send(g):
         for k in range(holders):
@@ -224,33 +229,33 @@
             control(g, holder)
             own_copy(g, holder).start()
 
-    def relay(g):
-        for k in range(holders):
-            holder = lax.rem(me + k, holders)
-            own_copy(g, holder).wait_recv()
-
-            @pl.when(has_target)
-            def _():
-                relay_copy(g, holder).start()
+    def relay_one(g, holder):
+        own_copy(g, holder).wait_recv()
+
+        @pl.when(has_target)
+        def _():
+            relay_copy(g, holder).start()
+
+    def relay(g, first=0):
+        for k in range(first, holders):
+            relay_one(g, lax.rem(me + k, holders))
 
     def mix(stack):
         mixed = jnp.dot(weights[...], stack, preferred_element_type=F32)
         return mixed[:block] + mixed[block:]
 
-    def mix_tails():
+    def mix_tails(q):
         @pl.when(has_source)
         def _():
-            for q in range(quads):
-                for holder in range(holders):
-                    relay_tail(q, holder).wait_recv()
-
-        for q in range(quads):
-            stack = jnp.concatenate(
-                [buf[q].reshape(block, LANES) for buf in (ctail, dtail, rtail)], axis=0
-            )
-            mixed = mix(stack)
-            for j in range(share):
-                last[q * share + j] = mixed[:, j * rest:(j + 1) * rest]
+            for holder in range(holders):
+                relay_tail(q, holder).wait_recv()
+
+        stack = jnp.concatenate(
+            [buf[q].reshape(block, LANES) for buf in (ctail, dtail, rtail)], axis=0
+        )
+        mixed = mix(stack)
+        for j in range(share):
+            last[q * share + j] = mixed[:, j * rest:(j + 1) * rest]
 
     def process(g):
         @pl.when(has_source)
@@ -290,22 +295,30 @@
         if first < last:
             lax.fori_loop(first, last, step, 0)
 
-    stage(early, early + 1, True, False, False)
+    relay_one(0, me)
+    convert(early)
+    send(early)
+    relay_one(1, me)
+    convert(early + 1)
+    relay(0, 1)
+    send_tails(0)
+    send(early + 1)
+    relay(1, 1)
+    total[...] = jnp.zeros_like(total)
     fill_mixing(weights, owner, holders, held_levels, rows, 1 - 2 * parity)
-    relay(0)
-    stage(early + 1, 2 * AHEAD, True, True, False)
-    for q in range(quads):
-        for holder in range(holders):
-            own_tail(q, holder).wait_recv()
-
-            @pl.when(has_target)
-            def _():
-                relay_tail(q, holder).start()
-
-    stage(2 * AHEAD, AHEAD + LAG + 1, True, True, False)
-    mix_tails()
+    lax.fori_loop(early + 2, pairs, convert, 0)
+    for q in range(1, quads):
+        send_tails(q)
+    stage(2 * AHEAD, 2 * AHEAD + 1, True, True, False)
+    pass_tails(0)
+    stage(2 * AHEAD + 1, AHEAD + LAG + 1, True, True, False)
+    for q in range(1, quads):
+        pass_tails(q)
+    mix_tails(0)
     process(0)
     stage(AHEAD + LAG + 1, pairs, True, True, True)
+    for q in range(1, quads):
+        mix_tails(q)
     stage(pairs, pairs + AHEAD, False, True, True)
     stage(pairs + AHEAD, pairs + AHEAD + LAG, False, False, True)
 

time: 28.3 us -> 28.3 us (level)
  no operation moved by 1% of the time
where the time goes in v9:
time: 28.3 us; the launch traced here: 28.1 us
  Pallas kernels  26.8 us (95%)
  local copies, waits for them, and re-layouts  1.3 us (5%)
    pallas_call x1, Pallas kernels, local(): pl.pallas_call(kernel, out_shape=jax.ShapeDtypeStruct(part, F32), in_spec...  26.8 us
    unnamed x3, local copies, waits for them, and re-layouts  1.3 us

profile of v9, /device:TPU:25, one launch (start us, length us, event | category | flops | bytes accessed | tf_op | source)
XLA Modules:
  0.0 28.1 jit_solution(10840430678109646544)
XLA Ops:
  0.0 0.0 copy-start
  0.0 0.7 %copy-done = s32[4]{0:T(128)S(1)} copy-done((s32[4]{0:T(128)S(1)}, s32[4]{0:T(128)}, u32[]{:S(2)}) %copy-start) | copy-done | bytes 40
  0.7 26.8 %shard_map.37 = f32[2,2,4,1440]{3,2,1,0:T(4,128)S(1)} custom-call(s32[4]{0:T(128)S(1)} %copy-done, bf16[16,2,4,4,1440]{4,3,2,1,0:T(4,128)(2,1)} %fields.1, f32[2,2,4,1440]{3,2,1,0:T(4,128)} %held_far.1), custom_call_target="tpu_custom_call" | custom-call | tf_op jit(solution)/shard_map/pallas_call | solution.py:387
  27.5 0.6 %copy.5 = f32[2,2,4,1440]{3,2,1,0:T(4,128)} copy(f32[2,2,4,1440]{3,2,1,0:T(4,128)S(1)} %shard_map.37) | data formatting | bytes 184320
Async XLA Ops:
  0.0 0.7 %copy-start = (s32[4]{0:T(128)S(1)}, s32[4]{0:T(128)}, u32[]{:S(2)}) copy-start(s32[4]{0:T(128)} %owner.1) | copy-start | bytes 52

commit v10 on v9

--- a/solution.py
+++ b/solution.py
@@ -13,7 +13,7 @@
 LANES = 128
 PAIR = 2
 AHEAD = 2
-LAG = 3
+LAG = 4
 F32 = jnp.float32
 BF16 = jnp.bfloat16
 

time: 28.3 us -> 28 us (0.989)
  no operation moved by 1% of the time
where the time goes in v10:
time: 28 us; the launch traced here: 27.9 us
  Pallas kernels  26.6 us (95%)
  local copies, waits for them, and re-layouts  1.3 us (5%)
    pallas_call x1, Pallas kernels, local(): pl.pallas_call(kernel, out_shape=jax.ShapeDtypeStruct(part, F32), in_spec...  26.6 us
    unnamed x3, local copies, waits for them, and re-layouts  1.3 us

profile of v10, /device:TPU:25, one launch (start us, length us, event | category | flops | bytes accessed | tf_op | source)
XLA Modules:
  0.0 27.9 jit_solution(1729365192939830837)
XLA Ops:
  0.0 0.0 copy-start
  0.0 0.7 %copy-done = s32[4]{0:T(128)S(1)} copy-done((s32[4]{0:T(128)S(1)}, s32[4]{0:T(128)}, u32[]{:S(2)}) %copy-start) | copy-done | bytes 40
  0.7 26.6 %shard_map.37 = f32[2,2,4,1440]{3,2,1,0:T(4,128)S(1)} custom-call(s32[4]{0:T(128)S(1)} %copy-done, bf16[16,2,4,4,1440]{4,3,2,1,0:T(4,128)(2,1)} %fields.1, f32[2,2,4,1440]{3,2,1,0:T(4,128)} %held_far.1), custom_call_target="tpu_custom_call" | custom-call | tf_op jit(solution)/shard_map/pallas_call | solution.py:387
  27.2 0.6 %copy.5 = f32[2,2,4,1440]{3,2,1,0:T(4,128)} copy(f32[2,2,4,1440]{3,2,1,0:T(4,128)S(1)} %shard_map.37) | data formatting | bytes 184320
Async XLA Ops:
  0.0 0.7 %copy-start = (s32[4]{0:T(128)S(1)}, s32[4]{0:T(128)}, u32[]{:S(2)}) copy-start(s32[4]{0:T(128)} %owner.1) | copy-start | bytes 52

commit v11 on v10

--- a/solution.py
+++ b/solution.py
@@ -284,10 +284,12 @@
 
     def stage(first, last, send_on, relay_on, process_on):
         def step(g, carry):
+            if relay_on:
+                relay_one(g - AHEAD, me)
             if send_on:
                 send(g)
             if relay_on:
-                relay(g - AHEAD)
+                relay(g - AHEAD, 1)
             if process_on:
                 process(g - AHEAD - LAG)
             return carry

time: 28 us -> 28 us (level)
  no operation moved by 1% of the time
where the time goes in v11:
time: 28 us; the launch traced here: 27.9 us
  Pallas kernels  26.6 us (95%)
  local copies, waits for them, and re-layouts  1.3 us (5%)
    pallas_call x1, Pallas kernels, local(): pl.pallas_call(kernel, out_shape=jax.ShapeDtypeStruct(part, F32), in_spec...  26.6 us
    unnamed x3, local copies, waits for them, and re-layouts  1.3 us

profile of v11, /device:TPU:25, one launch (start us, length us, event | category | flops | bytes accessed | tf_op | source)
XLA Modules:
  0.0 27.9 jit_solution(4387032003468280392)
XLA Ops:
  0.0 0.0 copy-start
  0.0 0.7 %copy-done = s32[4]{0:T(128)S(1)} copy-done((s32[4]{0:T(128)S(1)}, s32[4]{0:T(128)}, u32[]{:S(2)}) %copy-start) | copy-done | bytes 40
  0.7 26.6 %shard_map.37 = f32[2,2,4,1440]{3,2,1,0:T(4,128)S(1)} custom-call(s32[4]{0:T(128)S(1)} %copy-done, bf16[16,2,4,4,1440]{4,3,2,1,0:T(4,128)(2,1)} %fields.1, f32[2,2,4,1440]{3,2,1,0:T(4,128)} %held_far.1), custom_call_target="tpu_custom_call" | custom-call | tf_op jit(solution)/shard_map/pallas_call | solution.py:389
  27.2 0.6 %copy.5 = f32[2,2,4,1440]{3,2,1,0:T(4,128)} copy(f32[2,2,4,1440]{3,2,1,0:T(4,128)S(1)} %shard_map.37) | data formatting | bytes 184320
Async XLA Ops:
  0.0 0.7 %copy-start = (s32[4]{0:T(128)S(1)}, s32[4]{0:T(128)}, u32[]{:S(2)}) copy-start(s32[4]{0:T(128)} %owner.1) | copy-start | bytes 52

commit v12 on v11

--- a/solution.py
+++ b/solution.py
@@ -13,7 +13,7 @@
 LANES = 128
 PAIR = 2
 AHEAD = 2
-LAG = 4
+LAG = 3
 F32 = jnp.float32
 BF16 = jnp.bfloat16
 

time: 28 us -> 28.3 us (1.011)
  no operation moved by 1% of the time
where the time goes in v12:
time: 28.3 us; the launch traced here: 28.1 us
  Pallas kernels  26.8 us (95%)
  local copies, waits for them, and re-layouts  1.3 us (5%)
    pallas_call x1, Pallas kernels, local(): pl.pallas_call(kernel, out_shape=jax.ShapeDtypeStruct(part, F32), in_spec...  26.8 us
    unnamed x3, local copies, waits for them, and re-layouts  1.3 us

profile of v12, /device:TPU:25, one launch (start us, length us, event | category | flops | bytes accessed | tf_op | source)
XLA Modules:
  0.0 28.1 jit_solution(10672561630597937512)
XLA Ops:
  0.0 0.0 copy-start
  0.0 0.7 %copy-done = s32[4]{0:T(128)S(1)} copy-done((s32[4]{0:T(128)S(1)}, s32[4]{0:T(128)}, u32[]{:S(2)}) %copy-start) | copy-done | bytes 40
  0.7 26.8 %shard_map.37 = f32[2,2,4,1440]{3,2,1,0:T(4,128)S(1)} custom-call(s32[4]{0:T(128)S(1)} %copy-done, bf16[16,2,4,4,1440]{4,3,2,1,0:T(4,128)(2,1)} %fields.1, f32[2,2,4,1440]{3,2,1,0:T(4,128)} %held_far.1), custom_call_target="tpu_custom_call" | custom-call | tf_op jit(solution)/shard_map/pallas_call | solution.py:389
  27.5 0.6 %copy.5 = f32[2,2,4,1440]{3,2,1,0:T(4,128)} copy(f32[2,2,4,1440]{3,2,1,0:T(4,128)S(1)} %shard_map.37) | data formatting | bytes 184320
Async XLA Ops:
  0.0 0.7 %copy-start = (s32[4]{0:T(128)S(1)}, s32[4]{0:T(128)}, u32[]{:S(2)}) copy-start(s32[4]{0:T(128)} %owner.1) | copy-start | bytes 52
